TPU v7x, 128 devices: a whole 4x4x4 slice. The times are simulated.
128 devices in a mesh: history: 16 (over z, y), dp: 8 (over x, core).
Axes of the slice: x: 4, y: 4, z: 4, core: 2. Of those that a mesh axis runs over, the one named last changes fastest.
Arguments:
- actions: bfloat16 [16, 8, 128, 2048], P('history', 'dp'), may hold values from -6 to 6
- cotangent: bfloat16 [16, 8, 128, 2048], P('history', 'dp'), may hold values from -6 to 6
- cache_kv: bfloat16 [2, 16, 8, 512, 2048], P(None, None, 'dp', 'history'), may hold values from -6 to 6
- cache_len: int32 [16, 8], P('history', 'dp'), may hold values from 64 to 512, as said below
- cache_bucket: int32 [16, 8, 512], P(None, 'dp', 'history'), may hold values from 0 to 127
- new_bucket: int32 [16, 8, 128], P('history', 'dp'), may hold values from 0 to 127
- ln_gain: float32 [2048], replicated, may hold values from 0.5 to 1.5
- norm_gain: float32 [2048], replicated, may hold values from 0.5 to 1.5
- w_frozen: bfloat16 [3, 2048, 2048], P(None, None, 'dp'), may hold values from -0.125 to 0.125
- w_query: bfloat16 [2048, 2048], P(None, 'dp'), may hold values from -0.125 to 0.125
- query_m: float32 [2048, 2048], P(None, 'dp'), may hold values from -6 to 6
- query_v: float32 [2048, 2048], P(None, 'dp'), may hold values from 0.1 to 10
- w_out: bfloat16 [2048, 2048], P(None, 'dp'), may hold values from -0.125 to 0.125
- rab_table: float32 [16, 128], replicated, may hold values from -6 to 6
- rab_m: float32 [16, 128], replicated, may hold values from -6 to 6
- rab_v: float32 [16, 128], replicated, may hold values from 0.1 to 10
Outputs:
- output: bfloat16 [16, 8, 128, 2048], P('history', 'dp')
- query_new: bfloat16 [2048, 2048], P(None, 'dp')
- query_m_new: float32 [2048, 2048], P(None, 'dp')
- query_v_new: float32 [2048, 2048], P(None, 'dp')
- rab_new: float32 [16, 128], replicated
- rab_m_new: float32 [16, 128], replicated
- rab_v_new: float32 [16, 128], replicated
Inputs may be any that keep to these rules, and one draw needn't show every extreme that they name: `cache_len`: each user has between 64 and 512 valid cached actions; in every draw some user has exactly 512.
All inputs are finite; a program needn't handle non-finite values.
Results may differ from a plain program's by a relative error of at most 0.0094.
Values may be sent and summed in bfloat16 or wider, within the bound.
A program may use at most 128 MiB of HBM per device.

v0:
```python
import jax
import jax.numpy as jnp
from jax import lax
from jax.sharding import PartitionSpec as P

BETA_ONE = 0.9
BETA_TWO = 0.95
LEARN_RATE = 0.001
ADAM_EPS = 1e-08
NORM_EPS = 1e-05


def layer_norm(values, scaling):
    center = values - jnp.mean(values, axis=-1, keepdims=True)
    inverse = lax.rsqrt(jnp.mean(center * center, axis=-1, keepdims=True) + NORM_EPS)
    return center * inverse * scaling


def silu_slope(values):
    sigmoid = jax.nn.sigmoid(values)
    return sigmoid * (1.0 + values * (1.0 - sigmoid))


def adam_update(weight, moment_one, moment_two, gradient):
    first_new = BETA_ONE * moment_one + (1.0 - BETA_ONE) * gradient
    second_new = BETA_TWO * moment_two + (1.0 - BETA_TWO) * gradient * gradient
    stepped = weight.astype(jnp.float32) - LEARN_RATE * first_new / (
        jnp.sqrt(second_new) + ADAM_EPS
    )
    return (stepped.astype(weight.dtype), first_new, second_new)


def shards(
    actions,
    cotangent,
    cache_kv,
    cache_len,
    cache_bucket,
    new_bucket,
    ln_gain,
    norm_gain,
    w_frozen,
    w_query,
    query_m,
    query_v,
    w_out,
    rab_table,
    rab_m,
    rab_v,
):
    tok_rows = actions.shape[2]
    model_width = actions.shape[3]
    head_count = rab_table.shape[0]
    bucket_count = rab_table.shape[1]
    head_width = model_width // head_count
    score_scale = head_width ** (-0.5)
    highest = lax.Precision.HIGHEST
    x_float = actions.reshape(tok_rows, model_width).astype(jnp.float32)
    normed = layer_norm(x_float, ln_gain).astype(jnp.bfloat16)
    group_rows = lax.all_gather(normed, "dp", axis=0, tiled=True)
    query_pre = jnp.dot(group_rows, w_query, preferred_element_type=jnp.float32)
    frozen_pre = jnp.einsum("gd,jdc->gjc", group_rows, w_frozen, preferred_element_type=jnp.float32)
    stacked = jax.nn.silu(jnp.concatenate([query_pre[:, None, :], frozen_pre], axis=1)).astype(
        jnp.bfloat16
    )
    projected = lax.all_to_all(stacked, "dp", split_axis=0, concat_axis=2, tiled=True)
    query_heads = projected[:, 0, :].reshape(tok_rows, head_count, head_width)
    gate_float = projected[:, 1, :].astype(jnp.float32)
    value_new = projected[:, 2, :].reshape(tok_rows, head_count, head_width)
    key_new = projected[:, 3, :].reshape(tok_rows, head_count, head_width)
    bucket_shard = cache_bucket.reshape(1, cache_bucket.shape[0], 1, cache_bucket.shape[2])
    own_cache, own_bucket = (
        lax.all_to_all(cache_kv, "history", split_axis=1, concat_axis=3, tiled=True),
        lax.all_to_all(bucket_shard, "history", split_axis=1, concat_axis=3, tiled=True),
    )
    longest = own_cache.shape[3]
    keys_cache = own_cache[0].reshape(longest, head_count, head_width)
    values_cache = own_cache[1].reshape(longest, head_count, head_width)
    bucket_cache = own_bucket.reshape(longest)
    length = cache_len.reshape(())
    key_total = (length + tok_rows).astype(jnp.float32)
    key_block = 128
    block_total = (length + key_block - 1) // key_block
    levels = jnp.arange(bucket_count, dtype=jnp.int32)

    def block_terms(keys_part, values_part, bucket_ids, visible):
        onehot = (levels[:, None] == bucket_ids[None, :]).astype(jnp.float32)
        key_bias = jnp.dot(rab_table, onehot, precision=highest)
        scores = (
            jnp.einsum("thd,khd->htk", query_heads, keys_part, preferred_element_type=jnp.float32)
            * score_scale
            + key_bias[:, None, :]
        )
        return (keys_part, values_part, onehot, visible, scores)

    def cache_block(block_index):
        first_row = block_index * key_block
        keys_part = lax.dynamic_slice_in_dim(keys_cache, first_row, key_block, 0)
        values_part = lax.dynamic_slice_in_dim(values_cache, first_row, key_block, 0)
        bucket_ids = lax.dynamic_slice_in_dim(bucket_cache, first_row, key_block, 0)
        visible = (first_row + jnp.arange(key_block, dtype=jnp.int32) < length)[None, None, :]
        return block_terms(keys_part, values_part, bucket_ids, visible)

    positions = jnp.arange(tok_rows, dtype=jnp.int32)
    causal = (positions[None, :] <= positions[:, None])[None, :, :]
    new_block = block_terms(key_new, value_new, new_bucket.reshape(tok_rows), causal)

    def forward_part(block_parts):
        keys_part, values_part, onehot, visible, scores = block_parts
        weights = (jnp.where(visible, jax.nn.silu(scores), 0.0) / key_total).astype(jnp.bfloat16)
        return jnp.einsum("htk,khd->thd", weights, values_part, preferred_element_type=jnp.float32)

    attended = lax.fori_loop(
        0,
        block_total,
        lambda block_index, running: running + forward_part(cache_block(block_index)),
        forward_part(new_block),
    )
    attended = attended.reshape(tok_rows, model_width)
    nhat = layer_norm(attended, 1.0)
    gated = (nhat * norm_gain * gate_float).astype(jnp.bfloat16)
    whole_out = lax.all_gather(w_out, "dp", axis=1, tiled=True)
    projected_out = jnp.dot(gated, whole_out, preferred_element_type=jnp.float32)
    result = (projected_out + x_float).astype(jnp.bfloat16).reshape(actions.shape)
    grad_out = cotangent.reshape(tok_rows, model_width)
    grad_gated = jnp.einsum("tc,dc->td", grad_out, whole_out, preferred_element_type=jnp.float32)
    grad_hat = grad_gated * gate_float * norm_gain
    center = attended - jnp.mean(attended, axis=-1, keepdims=True)
    inverse = lax.rsqrt(jnp.mean(center * center, axis=-1, keepdims=True) + NORM_EPS)
    grad_att = inverse * (
        grad_hat
        - jnp.mean(grad_hat, axis=-1, keepdims=True)
        - nhat * jnp.mean(grad_hat * nhat, axis=-1, keepdims=True)
    )
    grad_heads = grad_att.astype(jnp.bfloat16).reshape(tok_rows, head_count, head_width)

    def backward_part(block_parts):
        keys_part, values_part, onehot, visible, scores = block_parts
        grad_weights = jnp.einsum(
            "thd,khd->htk", grad_heads, values_part, preferred_element_type=jnp.float32
        )
        grad_scores = jnp.where(visible, grad_weights * silu_slope(scores), 0.0) / key_total
        grad_query = (
            jnp.einsum(
                "htk,khd->thd",
                grad_scores.astype(jnp.bfloat16),
                keys_part,
                preferred_element_type=jnp.float32,
            )
            * score_scale
        )
        grad_table = jnp.dot(jnp.sum(grad_scores, axis=1), onehot.T, precision=highest)
        return (grad_query, grad_table)

    def backward_step(block_index, running):
        query_part, table_part = backward_part(cache_block(block_index))
        return (running[0] + query_part, running[1] + table_part)

    grad_query, grad_table = lax.fori_loop(0, block_total, backward_step, backward_part(new_block))
    grad_query = grad_query.reshape(tok_rows, model_width)
    query_columns = lax.all_to_all(grad_query, "dp", split_axis=1, concat_axis=0, tiled=True)
    grad_pre = (query_columns * silu_slope(query_pre)).astype(jnp.bfloat16)
    grad_weight = jnp.einsum("gd,gc->dc", group_rows, grad_pre, preferred_element_type=jnp.float32)
    grad_table = lax.psum(grad_table, ("history", "dp"))
    grad_sum = lax.psum(grad_weight, "history")
    query_new, query_m_new, query_v_new = adam_update(w_query, query_m, query_v, grad_sum)
    rab_new, rab_m_new, rab_v_new = adam_update(rab_table, rab_m, rab_v, grad_table)
    return (result, query_new, query_m_new, query_v_new, rab_new, rab_m_new, rab_v_new)


def solution(mesh):
    placed = (
        P("history", "dp", None, None),
        P("history", "dp", None, None),
        P(None, None, "dp", "history", None),
        P("history", "dp"),
        P(None, "dp", "history"),
        P("history", "dp", None),
        P(),
        P(),
        P(None, None, "dp"),
        P(None, "dp"),
        P(None, "dp"),
        P(None, "dp"),
        P(None, "dp"),
        P(),
        P(),
        P(),
    )
    return jax.shard_map(
        shards,
        mesh=mesh,
        in_specs=placed,
        out_specs=(
            P("history", "dp", None, None),
            P(None, "dp"),
            P(None, "dp"),
            P(None, "dp"),
            P(),
            P(),
            P(),
        ),
        check_vma=False,
    )
```

profile of v0, /device:TPU:0, one launch (start us, length us, event | category | flops | bytes accessed | tf_op | source)
XLA Modules:
  0.0 330.9 jit_solution(8666027582412598985)
XLA Ops:
  7.2 1.3 convert_reduce_fusion
  8.6 1.3 fusion.50
  9.9 2.2 fusion.52
  12.2 0.7 all-gather.5.cloned.1.call-update
  12.9 8.1 %all-to-all-start.2 = ((s32[1,16,1,32]{3,2,0,1:T(1,128)}), s32[1,16,1,32]{3,2,0,1:T(1,128)S(1)}, u32[]{:S(2)}, u32[]{:S(2)}) async-start(s32[1,16,1,32]{3,2,0,1:T(1,128)} %bitcast.12), calls=%async_computation.2 | async-start | bytes 16384 | tf_op jit(solution)/shard_map/all_to_all | solution.py:74
  21.1 4.7 %copy.67 = bf16[2,16,1,32,2048]{4,3,2,0,1:T(8,128)(2,1)} copy(bf16[2,16,1,32,2048]{4,3,2,1,0:T(8,128)(2,1)} %param.22) | data formatting | bytes 8388608 | tf_op args[2]
  25.8 2.8 all-to-all-done.2
  28.5 4.6 %all-to-all-start.1 = ((bf16[2,16,1,32,2048]{4,3,2,0,1:T(8,128)(2,1)}), bf16[2,16,1,32,2048]{4,3,2,0,1:T(8,128)(2,1)}, u32[]{:S(2)}, u32[]{:S(2)}) async-start(bf16[2,16,1,32,2048]{4,3,2,0,1:T(8,128)(2,1)} %copy.67), calls=%async_computation.1 | async-start | bytes 8388608 | tf_op jit(solution)/shard_map/all_to_all | solution.py:73
  33.1 13.7 %all-gather.3.cloned.1.call-done = bf16[1024,2048]{1,0:T(8,128)(2,1)} async-done(((bf16[128,2048]{1,0:T(8,128)(2,1)}), bf16[1024,2048]{1,0:T(8,128)(2,1)}) %all-gather.3.cloned.1.call-update) | async-done | bytes 4194320 | tf_op jit(solution)/shard_map/all_gather | solution.py:60
  46.9 3.9 %fusion.79 = f32[1024,256]{1,0:T(8,128)S(1)} fusion(bf16[1024,2048]{1,0:T(8,128)(2,1)} %all-gather.3.cloned.1.call-done, bf16[2048,256]{1,0:T(8,128)(2,1)} %param.29), kind=kOutput, calls=%fused_computation.123 | convolution fusion | flops 1073741824 | bytes 6291456 | tf_op jit(solution)/shard_map/dot_general | solution.py:61
  50.8 3.4 %fusion.37 = f32[1024,3,256]{2,0,1:T(8,128)S(1)} fusion(bf16[3,2048,256]{2,1,0:T(8,128)(2,1)S(1)} %copy-done, bf16[1024,2048]{1,0:T(8,128)(2,1)S(1)} %copy-done.18), kind=kOutput, calls=%fused_computation.49 | convolution fusion | flops 3221225472 | bytes 10485760 | tf_op jit(solution)/shard_map/gd,jdc->gjc/dot_general | solution.py:62
  54.2 1.1 multiply_convert_fusion
  55.3 2.9 copy.60
  58.3 36.3 %all-to-all-done.1 = bf16[2,16,1,32,2048]{4,3,2,0,1:T(8,128)(2,1)} async-done(((bf16[2,16,1,32,2048]{4,3,2,0,1:T(8,128)(2,1)}), bf16[2,16,1,32,2048]{4,3,2,0,1:T(8,128)(2,1)}, u32[]{:S(2)}, u32[]{:S(2)}) %all-to-all-start.1) | async-done | bytes 4194336 | tf_op jit(solution)/shard_map/all_to_all | solution.py:73
  94.5 4.4 %all-to-all-start = ((bf16[1024,4,256]{2,1,0:T(4,128)(2,1)}), bf16[1024,4,256]{2,1,0:T(4,128)(2,1)}, u32[]{:S(2)}, u32[]{:S(2)}) async-start(bf16[1024,4,256]{2,1,0:T(4,128)(2,1)} %copy.60), calls=%async_computation | async-start | bytes 4194304 | tf_op jit(solution)/shard_map/all_to_all | solution.py:66
  100.0 0.5 broadcast.149
  100.5 0.7 reduce.6
  101.2 2.8 fusion.76
  104.0 0.6 copy.92
  104.7 0.5 copy.69
  105.2 2.0 copy.91
  107.2 18.9 %all-to-all-done = bf16[1024,4,256]{2,1,0:T(4,128)(2,1)} async-done(((bf16[1024,4,256]{2,1,0:T(4,128)(2,1)}), bf16[1024,4,256]{2,1,0:T(4,128)(2,1)}, u32[]{:S(2)}, u32[]{:S(2)}) %all-to-all-start) | async-done | bytes 2097184 | tf_op jit(solution)/shard_map/all_to_all | solution.py:66
  126.1 4.1 %copy.104 = bf16[8,128,4,256]{3,0,1,2:T(8,128)(2,1)} copy(bf16[8,128,4,256]{3,2,1,0:T(4,128)(2,1)} %bitcast.3) | data formatting | bytes 4194304 | tf_op jit(solution)/shard_map/all_to_all | solution.py:66
  130.2 4.2 %all_to_all.44 = bf16[128,4,2048]{2,0,1:T(8,128)(2,1)} reshape(bf16[128,4,8,256]{3,2,0,1:T(8,128)(2,1)} %bitcast.164) | data formatting | bytes 4194304 | tf_op jit(solution)/shard_map/all_to_all | solution.py:66
  134.4 2.5 fusion.77
  136.9 1.3 copy.63
  138.2 2.1 copy.64
  140.2 1.0 copy.62
  141.5 1.4 fusion.44
  143.0 1.5 convolution_bitcast_fusion.4
  144.5 10.0 %while.24 = (s32[]{:T(128)}, f32[128,16,128]{0,2,1:T(8,128)}, s32[]{:T(128)}, bf16[512,16,128]{2,1,0:T(8,128)(2,1)}, s32[]{:T(128)}, /*index=5*/bf16[512,16,128]...) while((s32[]{:T(128)}, f32[128,16,128]{0,2,1:T(8,128)}, ...), condition=%wide.region_3.4_spmd.clone, body=%wide.region_2.3_spmd.clone.sunk | while | flops 140001536 | bytes 4745547 | solution.py:113
  144.7 1.1 constant_dynamic-slice_fusion.4
  145.8 0.7 add_compare_fusion.4
  146.5 3.0 fusion.125
  149.7 1.1 constant_dynamic-slice_fusion.4
  150.8 0.7 add_compare_fusion.4
  151.5 3.0 fusion.125
  154.5 2.3 reduce_sum.82
  156.9 1.6 copy.87
  158.4 1.5 multiply_reduce_fusion.1
  160.0 6.7 %fusion.72 = (f32[128]{0:T(128)S(1)}, f32[128]{0:T(128)S(1)}, f32[128,2048]{1,0:T(8,128)S(1)}) fusion(f32[128]{0:T(128)S(1)} %add_rsqrt_fusion, f32[128,2048]{1,0:T(8,128)S(1)} %copy.87, f32[128]{0:T(128)S(1)} %broadcast_multiply_fusion.2, f32[2048]{0:T(1024)S(1)} %copy-done.14, bf16[128,4,2048]{2,0,1:T(8,128)(2,1)} %all_to_all.44, ...), kind=kOutput, calls=%fused_computation.118 | convolution fusion | flops 1075838720 | bytes 11544576 | tf_op jit(solution)/shard_map/tc,dc->td/dot_general | solution.py:126
  166.7 1.3 copy_bitcast_fusion.1
  168.0 0.8 fusion.78
  169.1 0.5 fusion.43
  170.0 12.1 %while.25 = (s32[]{:T(128)}, f32[128,16,128]{2,0,1:T(8,128)S(1)}, f32[16,128]{1,0:T(8,128)S(1)}, s32[]{:T(128)}, bf16[512,16,128]{2,0,1:T(8,128)(2,1)}, /*index=...) while((s32[]{:T(128)}, f32[128,16,128]{2,0,1:T(8,128)S(1)}, ...), condition=%wide.region_11.12_spmd.clone, body=%wide.region_9.11_spmd.clone.sunk | while | flops 211845376 | bytes 11069947 | solution.py:159
  170.4 1.7 fusion.133
  172.2 1.1 constant_dynamic-slice_fusion.5
  173.2 0.7 add_compare_fusion.5
  173.9 0.7 fusion.134
  174.6 1.4 fusion.135
  176.4 1.7 fusion.133
  178.1 1.1 constant_dynamic-slice_fusion.5
  179.2 0.7 add_compare_fusion.5
  179.9 0.7 fusion.134
  180.6 1.4 fusion.135
  182.1 0.4 copy.79
  182.5 39.6 %all_to_all.55 = f32[128,8,256]{0,2,1:T(8,128)} all-to-all(f32[128,8,256]{0,2,1:T(8,128)S(1)} %bitcast.171), channel_id=1, replica_groups=mesh['history'=16,'dp'=8] {'dp'}, dimensions={1} | all-to-all | bytes 2097152 | tf_op jit(solution)/shard_map/all_to_all | solution.py:161
  222.1 1.6 copy.80
  224.2 4.8 %fusion.80 = f32[2048,256]{1,0:T(8,128)} fusion(bf16[1024,2048]{1,0:T(8,128)(2,1)} %all-gather.3.cloned.1.call-done, bf16[1024,256]{1,0:T(8,128)(2,1)S(1)} %fusion.54), kind=kOutput, calls=%fused_computation.124 | convolution fusion | flops 1073741824 | bytes 6815744 | tf_op jit(solution)/shard_map/gd,gc->dc/dot_general | solution.py:163
  229.0 66.0 %psum.15 = f32[16,128]{1,0:T(8,128)S(1)} all-reduce(f32[16,128]{1,0:T(8,128)S(1)} %get-tuple-element.136), channel_id=1, replica_groups=mesh['history'=16,'dp'=8] {'history','dp'}, use_global_device_ids=true, to_apply=%region_13.14 | all-reduce | flops 2048 | bytes 16384 | tf_op jit(solution)/shard_map/psum | solution.py:164
  295.0 0.6 divide_subtract_fusion
  295.6 5.7 %fusion.41 = bf16[1,1,128,2048]{3,2,1,0:T(8,128)(2,1)} fusion(bf16[2048,2048]{1,0:T(8,128)(2,1)} %all-gather.5.cloned.1.call-done, bf16[1,1,128,2048]{3,2,1,0:T(8,128)(2,1)S(1)} %copy-done.4, f32[128,2048]{1,0:T(8,128)S(1)} %copy.87, f32[2048]{0:T(1024)S(1)} %copy-done.14, f32[128]{0:T(128)S(1)} %add_rsqrt_fusion, f32[128]{0:T(128)S(1)} %broadcast_multiply_fusion.2, ...), kind=kOutput, calls=%fused_computation.57 | convolution fusion | flops 1076101120 | bytes 11019264 | tf_op jit(solution)/shard_map/dot_general | solution.py:123
  301.3 16.6 %all-reduce.2.cloned.1.call-done = f32[2048,256]{1,0:T(8,128)} async-done(((f32[2048,256]{1,0:T(8,128)}), f32[2048,256]{1,0:T(8,128)}) %all-reduce.2.cloned.1.call-update) | async-done | bytes 2097168 | tf_op jit(solution)/shard_map/psum | solution.py:165
  317.9 6.4 %subtract_convert_fusion = (bf16[2048,256]{1,0:T(8,128)(2,1)}, f32[2048,256]{1,0:T(8,128)}, f32[2048,256]{1,0:T(8,128)}) fusion(bf16[2048,256]{1,0:T(8,128)(2,1)} %param.29, f32[2048,256]{1,0:T(8,128)} %all-reduce.2.cloned.1.call-done, f32[2048,256]{1,0:T(8,128)} %param.30, f32[2048,256]{1,0:T(8,128)} %param.31), kind=kLoop, calls=%fused_computation.60 | loop fusion | flops 6815744 | bytes 12582912 | tf_op jit(solution)/shard_map/convert_element_type | solution.py:30
  (68 shorter events, 3.2 us)
Async XLA Ops:
  7.2 43.6 %copy-start = (bf16[3,2048,256]{2,1,0:T(8,128)(2,1)S(1)}, bf16[3,2048,256]{2,1,0:T(8,128)(2,1)}, u32[]{:S(2)}) copy-start(bf16[3,2048,256]{2,1,0:T(8,128)(2,1)} %param.28) | copy-start | bytes 9437188
  7.2 39.7 %all-gather.3.cloned.1.call-start = ((), (), s32[]{:S(2)}) async-start(), calls=%async_computation.4 | async-start | bytes 4718592 | tf_op jit(solution)/shard_map/all_gather | solution.py:60
  12.2 147.8 %all-gather.5.cloned.1.call-start = ((), (), s32[]{:S(2)}) async-start(), calls=%async_computation.5 | async-start | bytes 9437184 | tf_op jit(solution)/shard_map/all_gather | solution.py:122
  12.9 15.6 %all-to-all-start.2 = ((s32[1,16,1,32]{3,2,0,1:T(1,128)}), s32[1,16,1,32]{3,2,0,1:T(1,128)S(1)}, u32[]{:S(2)}, u32[]{:S(2)}) async-start(s32[1,16,1,32]{3,2,0,1:T(1,128)} %bitcast.12), calls=%async_computation.2 | async-start | bytes 16384 | tf_op jit(solution)/shard_map/all_to_all | solution.py:74
  28.5 66.0 %all-to-all-start.1 = ((bf16[2,16,1,32,2048]{4,3,2,0,1:T(8,128)(2,1)}), bf16[2,16,1,32,2048]{4,3,2,0,1:T(8,128)(2,1)}, u32[]{:S(2)}, u32[]{:S(2)}) async-start(bf16[2,16,1,32,2048]{4,3,2,0,1:T(8,128)(2,1)} %copy.67), calls=%async_computation.1 | async-start | bytes 8388608 | tf_op jit(solution)/shard_map/all_to_all | solution.py:73
  46.9 3.9 %copy-start.18 = (bf16[1024,2048]{1,0:T(8,128)(2,1)S(1)}, bf16[1024,2048]{1,0:T(8,128)(2,1)}, u32[]{:S(2)}) copy-start(bf16[1024,2048]{1,0:T(8,128)(2,1)} %all-gather.3.cloned.1.call-done) | copy-start | bytes 12582916
  50.8 3.4 %copy-start.6 = (f32[1024,256]{1,0:T(8,128)}, f32[1024,256]{1,0:T(8,128)S(1)}, u32[]{:S(2)}) copy-start(f32[1024,256]{1,0:T(8,128)S(1)} %fusion.79) | copy-start | bytes 3145732
  58.3 41.6 %copy-start.8 = (f32[16,128]{1,0:T(8,128)S(1)}, f32[16,128]{1,0:T(8,128)}, u32[]{:S(2)}) copy-start(f32[16,128]{1,0:T(8,128)} %param.33) | copy-start | bytes 24580
  58.3 41.6 %copy-start.17 = (s32[1,1,128]{2,1,0:T(1,128)S(1)}, s32[1,1,128]{2,1,0:T(1,128)}, u32[]{:S(2)}) copy-start(s32[1,1,128]{2,1,0:T(1,128)} %param.25) | copy-start | bytes 1540
  94.5 31.6 %all-to-all-start = ((bf16[1024,4,256]{2,1,0:T(4,128)(2,1)}), bf16[1024,4,256]{2,1,0:T(4,128)(2,1)}, u32[]{:S(2)}, u32[]{:S(2)}) async-start(bf16[1024,4,256]{2,1,0:T(4,128)(2,1)} %copy.60), calls=%async_computation | async-start | bytes 4194304 | tf_op jit(solution)/shard_map/all_to_all | solution.py:66
  98.9 219.0 %all-reduce.2.cloned.1.call-start = ((), (), s32[]{:S(2)}) async-start(), calls=%async_computation.6 | async-start | bytes 4194304 | tf_op jit(solution)/shard_map/psum | solution.py:165
  141.5 1.5 copy-start.11
  143.0 1.5 copy-start.9
  154.5 2.3 copy-start.3
  154.5 5.4 %copy-start.2 = (bf16[512,16,128]{2,0,1:T(8,128)(2,1)}, bf16[512,16,128]{2,0,1:T(8,128)(2,1)S(1)}, u32[]{:S(2)}) copy-start(bf16[512,16,128]{2,0,1:T(8,128)(2,1)S(1)} %get-tuple-element.555) | copy-start | bytes 6291460
  154.5 5.5 %copy-start.14 = (f32[2048]{0:T(1024)S(1)}, f32[2048]{0:T(1024)}, u32[]{:S(2)}) copy-start(f32[2048]{0:T(1024)} %param.27) | copy-start | bytes 24580
  166.7 1.3 copy-start.10
  166.7 1.4 copy-start.12
  168.0 1.0 copy-start.5
  170.2 3.7 %copy-start.13 = (bf16[128,16,128]{2,0,1:T(8,128)(2,1)S(1)}, bf16[128,16,128]{2,0,1:T(8,128)(2,1)}, u32[]{:S(2)}) copy-start(bf16[128,16,128]{2,0,1:T(8,128)(2,1)} %get-tuple-element.542) | copy-start | bytes 1572868 | tf_op jit(solution)/shard_map/while
  176.1 3.7 %copy-start.13 = (bf16[128,16,128]{2,0,1:T(8,128)(2,1)S(1)}, bf16[128,16,128]{2,0,1:T(8,128)(2,1)}, u32[]{:S(2)}) copy-start(bf16[128,16,128]{2,0,1:T(8,128)(2,1)} %get-tuple-element.542) | copy-start | bytes 1572868 | tf_op jit(solution)/shard_map/while
  222.1 1.7 copy-start.7
  229.0 66.0 %copy-start.15 = (f32[16,128]{1,0:T(8,128)S(1)}, f32[16,128]{1,0:T(8,128)}, u32[]{:S(2)}) copy-start(f32[16,128]{1,0:T(8,128)} %param.34) | copy-start | bytes 24580
  229.0 66.0 %copy-start.16 = (f32[16,128]{1,0:T(8,128)S(1)}, f32[16,128]{1,0:T(8,128)}, u32[]{:S(2)}) copy-start(f32[16,128]{1,0:T(8,128)} %param.35) | copy-start | bytes 24580
  229.0 66.7 %copy-start.4 = (bf16[1,1,128,2048]{3,2,1,0:T(8,128)(2,1)S(1)}, bf16[1,1,128,2048]{3,2,1,0:T(8,128)(2,1)}, u32[]{:S(2)}) copy-start(bf16[1,1,128,2048]{3,2,1,0:T(8,128)(2,1)} %param.20) | copy-start | bytes 1572868
  317.9 6.4 %copy-start.1 = (bf16[3,2048,256]{2,1,0:T(8,128)(2,1)S(1)}, bf16[3,2048,256]{2,1,0:T(8,128)(2,1)}, u32[]{:S(2)}) copy-start(bf16[3,2048,256]{2,1,0:T(8,128)(2,1)} %param.28) | copy-start | bytes 9437188
Sparse Core Ops, SparseCore 0:
  12.3 34.5 all-gather.2
  48.5 53.9 all-gather.4
  229.1 88.7 all-reduce.1
where the time goes:
time: 333 us; the launch traced here: 331 us
  blocking collectives  106 us (32%)
  waiting for transfers between devices  89 us (27%)
  matrix products  43.4 us (13%)
  local copies, waits for them, and re-layouts  38.6 us (12%)
  other arithmetic  21.8 us (7%)
  starting transfers between devices  17.4 us (5%)
  between operations  14.7 us (4%)
    psum x1, blocking collectives, shards(): grad_table = lax.psum(grad_table, ('history', 'dp'))  66 us
    all_to_all x1, blocking collectives, shards(): lax.all_to_all(grad_query, 'dp', split_axis=1, concat_axis=0, tiled=True)  39.6 us
    all_to_all x1, waiting for transfers between devices, shards(): lax.all_to_all(cache_kv, 'history', split_axis=1, concat_axis=3, tiled=True)  36.3 us
    all_to_all x1, waiting for transfers between devices, shards(): lax.all_to_all(stacked, 'dp', split_axis=0, concat_axis=2, tiled=True)  18.9 us
    psum x1, waiting for transfers between devices, shards(): grad_sum = lax.psum(grad_weight, 'history')  16.6 us
    all_gather x1, waiting for transfers between devices, shards(): group_rows = lax.all_gather(normed, 'dp', axis=0, tiled=True)  13.7 us
    unnamed x42, local copies, waits for them, and re-layouts  8.78 us
    all_to_all x2, local copies, waits for them, and re-layouts, shards(): lax.all_to_all(stacked, 'dp', split_axis=0, concat_axis=2, tiled=True)  8.27 us
  transfers between devices with their start and end apart: 6, of which 5 were waited for; matrix products, arithmetic and copies ran while one was open for 18% of the time, Pallas kernels for 0%

commit v1 on v0

v1 whole, which is shorter than its diff:
```python
import functools

import jax
import jax.numpy as jnp
from jax import lax
from jax.experimental import pallas as pl
from jax.experimental.pallas import tpu as pltpu
from jax.sharding import PartitionSpec as P

BETA_ONE = 0.9
BETA_TWO = 0.95
LEARN_RATE = 0.001
ADAM_EPS = 1e-08
NORM_EPS = 1e-05

MESH = pl.DeviceIdType.MESH
F32 = jnp.float32
BF16 = jnp.bfloat16

TOK = 128
WIDTH = 2048
COLS = 256
HEAD = 128
HEADS = 16
BUCKETS = 128
HIST = 16
DP = 8
SLAB = 32
CACHED = HIST * SLAB
KEYS = CACHED + TOK
SCALE = HEAD ** (-0.5)


def adam_update(weight, moment_one, moment_two, gradient):
    first_new = BETA_ONE * moment_one + (1.0 - BETA_ONE) * gradient
    second_new = BETA_TWO * moment_two + (1.0 - BETA_TWO) * gradient * gradient
    stepped = weight.astype(F32) - LEARN_RATE * first_new / (jnp.sqrt(second_new) + ADAM_EPS)
    return (stepped.astype(weight.dtype), first_new, second_new)


def dot_nn(a, b):
    return jnp.dot(a, b, preferred_element_type=F32)


def dot_nt(a, b):
    return lax.dot_general(a, b, (((1,), (1,)), ((), ())), preferred_element_type=F32)


def three_parts(values):
    first = values.astype(BF16)
    rest = values - first.astype(F32)
    second = rest.astype(BF16)
    third = (rest - second.astype(F32)).astype(BF16)
    return first, second, third


def silu_slope(values):
    sigmoid = 0.5 * jnp.tanh(0.5 * values) + 0.5
    return sigmoid * (1.0 + values * (1.0 - sigmoid))


def kernel(
    act_hbm, cot_hbm, cache_hbm, length, bucket_hbm, new_bucket, ln_gain, norm_gain, frozen_hbm, query_hbm, wout_hbm, rab,
    out_ref, gsum_hbm, gtab_ref,
    act, cot, wts, rows, pre_slope, sent, proj, kv, bks, onehot, bias, att, slope, wout, grad_gated, gated, grad_att,
    tsum, gq_out, gq_in, grad_pre_t, rs_out, rs_in, ag_out, tab_one, tab_two,
    loc_sem, kv_s, kv_r, bk_s, bk_r, g_s, g_r, pj_s, pj_r, w_s, w_r, gq_s, gq_r, rs_s, rs_r, ag_s, ag_r, t1_s, t1_r, t2_s, t2_r,
):
    h = lax.axis_index("history")
    d = lax.axis_index("dp")
    z, y = h // 4, lax.rem(h, 4)
    x, c = d // 2, lax.rem(d, 2)

    def hist(k):
        return lax.rem(z + k // 4, 4) * 4 + lax.rem(y + lax.rem(k, 4), 4)

    def dpx(kx, kc):
        return lax.rem(x + kx, 4) * 2 + lax.rem(c + kc, 2)

    def dpo(k):
        return lax.rem(x + k // 2, 4) * 2 + lax.rem(c + lax.rem(k, 2), 2)

    barrier = pltpu.get_barrier_semaphore()

    def greet_hist(k, carry):
        pl.semaphore_signal(barrier, inc=1, device_id=(hist(k), d), device_id_type=MESH)
        return carry

    def greet_dp(k, carry):
        pl.semaphore_signal(barrier, inc=1, device_id=(h, dpo(k)), device_id_type=MESH)
        return carry

    lax.fori_loop(1, DP, greet_dp, 0)
    lax.fori_loop(1, HIST, greet_hist, 0)

    load_act = pltpu.make_async_copy(act_hbm, act, loc_sem.at[0])
    load_act.start()
    load_query = pltpu.make_async_copy(query_hbm, wts.at[0], loc_sem.at[1])
    load_query.start()
    load_frozen = pltpu.make_async_copy(frozen_hbm, wts.at[pl.ds(1, 3)], loc_sem.at[2])
    load_frozen.start()
    load_cot = pltpu.make_async_copy(cot_hbm, cot, loc_sem.at[3])
    load_cot.start()
    load_wout = pltpu.make_async_copy(wout_hbm, wout.at[d], loc_sem.at[4])
    load_wout.start()
    own_slab = kv.at[:, pl.ds(pl.multiple_of(h * SLAB, SLAB), SLAB), :]
    load_kv = pltpu.make_async_copy(cache_hbm.at[:, h], own_slab, loc_sem.at[5])
    load_kv.start()
    load_bk = pltpu.make_async_copy(bucket_hbm.at[h], bks.at[h], loc_sem.at[6])
    load_bk.start()

    load_act.wait()

    def norm_rows(r, carry):
        part = pl.ds(pl.multiple_of(r * 16, 16), 16)
        values = act[part, :].astype(F32)
        center = values - jnp.mean(values, axis=-1, keepdims=True)
        inverse = lax.rsqrt(jnp.mean(center * center, axis=-1, keepdims=True) + NORM_EPS)
        rows[d, part, :] = (center * inverse * ln_gain[...]).astype(BF16)
        return carry

    lax.fori_loop(0, TOK // 16, norm_rows, 0)
    pl.semaphore_wait(barrier, HIST - 1 + DP - 1)

    def remote(src, dst, send, recv, device):
        return pltpu.make_async_remote_copy(
            src_ref=src, dst_ref=dst, send_sem=send, recv_sem=recv, device_id=device, device_id_type=MESH
        )

    def ring_gather(buffer, half_rows, own, send, recv):
        right, left, sibling = (h, dpx(1, 0)), (h, dpx(3, 0)), (h, dpx(0, 1))
        low, high = pl.ds(0, half_rows), pl.ds(half_rows, half_rows)
        from_left, from_right, far = dpx(3, 0), dpx(1, 0), dpx(2, 0)
        specs = [
            (own, buffer.at[d], sibling),
            (own, buffer.at[d], right),
            (own, buffer.at[d], left),
            (buffer.at[from_left, low], buffer.at[from_left, low], right),
            (buffer.at[from_right, high], buffer.at[from_right, high], left),
            (buffer.at[from_left], buffer.at[from_left], sibling),
            (buffer.at[from_right], buffer.at[from_right], sibling),
            (buffer.at[far, low], buffer.at[far, low], sibling),
            (buffer.at[far, high], buffer.at[far, high], sibling),
        ]
        return [remote(s, t, send.at[i], recv.at[i], dev) for i, (s, t, dev) in enumerate(specs)]

    ring = ring_gather(rows, TOK // 2, rows.at[d], g_s, g_r)
    for i in (1, 2, 0):
        ring[i].start()

    def kv_copy(k):
        to = hist(k)
        return remote(cache_hbm.at[:, to], own_slab, kv_s.at[k], kv_r.at[k], (to, d))

    def bk_copy(k):
        to = hist(k)
        return remote(bucket_hbm.at[to], bks.at[h], bk_s.at[k], bk_r.at[k], (to, d))

    def send_cache(k, carry):
        bk_copy(k).start()
        kv_copy(k).start()
        return carry

    lax.fori_loop(1, HIST, send_cache, 0)

    def project(chip):
        part = pl.ds(pl.multiple_of(chip * 2, 2), 2)
        chip_rows = rows[part].reshape(2 * TOK, WIDTH)
        for j in range(4):
            pre = dot_nn(chip_rows, wts[j])
            sigmoid = 0.5 * jnp.tanh(0.5 * pre) + 0.5
            acted = pre * sigmoid
            if j == 0:
                pre_slope[part] = (sigmoid + acted * (1.0 - sigmoid)).reshape(2, TOK, COLS)
            sent[part, :, pl.ds(j * COLS, COLS)] = acted.astype(BF16).reshape(2, TOK, COLS)

    def pj_copy(k):
        to = dpo(k)
        return remote(sent.at[to], proj.at[d], pj_s.at[k], pj_r.at[k], (h, to))

    load_query.wait()
    load_frozen.wait()
    ring[0].wait_recv()
    project(x)
    pj_copy(1).start()
    own_proj = pltpu.make_async_copy(sent.at[d], proj.at[d], loc_sem.at[7])
    own_proj.start()
    ring[1].wait_recv()
    ring[3].start()
    ring[5].start()
    ring[2].wait_recv()
    ring[4].start()
    ring[6].start()
    ring[5].wait_recv()
    project(lax.rem(x + 3, 4))
    pj_copy(6).start()
    pj_copy(7).start()
    ring[6].wait_recv()
    project(lax.rem(x + 1, 4))
    pj_copy(2).start()
    pj_copy(3).start()
    ring[3].wait_recv()
    ring[7].start()
    ring[4].wait_recv()
    ring[8].start()
    ring[7].wait_recv()
    ring[8].wait_recv()
    project(lax.rem(x + 2, 4))
    pj_copy(4).start()
    pj_copy(5).start()

    wring = ring_gather(wout, WIDTH // 2, wout_hbm, w_s, w_r)
    for i in (1, 2, 0):
        wring[i].start()

    load_bk.wait()

    def wait_bk(k, carry):
        bk_copy(k).wait_recv()
        return carry

    lax.fori_loop(1, HIST, wait_bk, 0)
    levels = lax.broadcasted_iota(jnp.int32, (BUCKETS, TOK), 0)
    for q in range(4):
        ids = (bks[4 * q] + bks[4 * q + 1] + bks[4 * q + 2] + bks[4 * q + 3])[0:1, :]
        onehot[:, pl.ds(q * TOK, TOK)] = jnp.where(levels == ids, 1.0, 0.0).astype(BF16)
    onehot[:, pl.ds(CACHED, TOK)] = jnp.where(levels == new_bucket[...], 1.0, 0.0).astype(BF16)
    hot = onehot[...]
    bias_sum = jnp.zeros((HEADS, KEYS), F32)
    for term in reversed(three_parts(rab[...])):
        bias_sum = bias_sum + dot_nn(term, hot)
    bias[...] = bias_sum

    count = length[0, 0]
    share = 1.0 / jnp.full((1, TOK), count + TOK, jnp.int32).astype(F32)
    cached_pos = lax.broadcasted_iota(jnp.int32, (1, CACHED), 1)
    share_cached = jnp.where(cached_pos < count, jnp.concatenate([share] * 4, axis=1), 0.0)
    row_pos = lax.broadcasted_iota(jnp.int32, (TOK, TOK), 0)
    col_pos = lax.broadcasted_iota(jnp.int32, (TOK, TOK), 1)
    share_new = jnp.where(col_pos <= row_pos, jnp.broadcast_to(share, (TOK, TOK)), 0.0)

    def wait_pj(k, carry):
        pj_copy(k).wait_recv()
        return carry

    own_proj.wait()
    lax.fori_loop(1, DP, wait_pj, 0)

    def wait_kv(k, carry):
        kv_copy(k).wait_recv()
        return carry

    load_kv.wait()
    lax.fori_loop(1, HIST, wait_kv, 0)

    def attend(m, carry):
        for k in range(2):
            head = m * 2 + k
            lanes = pl.ds(pl.multiple_of(head * HEAD, HEAD), HEAD)
            query = proj[m, :, pl.ds(k * HEAD, HEAD)]
            value_new = proj[m, :, pl.ds(2 * COLS + k * HEAD, HEAD)]
            key_new = proj[m, :, pl.ds(3 * COLS + k * HEAD, HEAD)]
            key_bias = bias[pl.ds(head, 1), :]
            total = jnp.zeros((TOK, HEAD), F32)
            parts = (
                (kv[0, :, lanes], kv[1, :, lanes], pl.ds(0, CACHED), key_bias[:, :CACHED], share_cached),
                (key_new, value_new, pl.ds(CACHED, TOK), key_bias[:, CACHED:], share_new),
            )
            for keys, values, where, bias_part, share_part in parts:
                score = dot_nt(query, keys) * SCALE + bias_part
                sigmoid = 0.5 * jnp.tanh(0.5 * score) + 0.5
                weight = score * sigmoid * share_part
                slope[head, :, where] = sigmoid * share_part + weight * (1.0 - sigmoid)
                total = total + dot_nn(weight.astype(BF16), values)
            att[:, lanes] = total
        return carry

    lax.fori_loop(0, DP, attend, 0)

    load_cot.wait()
    load_wout.wait()

    def gated_part(m, first=False):
        lanes = pl.ds(pl.multiple_of(m * COLS, COLS), COLS)
        for n in range(4):
            cols = pl.ds(n * 512, 512)
            part = dot_nt(cot[:, lanes], wout[m, cols, :])
            grad_gated[:, cols] = part if first else grad_gated[:, cols] + part

    gated_part(d, True)
    wring[1].wait_recv()
    wring[3].start()
    wring[5].start()
    wring[2].wait_recv()
    wring[4].start()
    wring[6].start()
    wring[0].wait_recv()
    gated_part(dpx(0, 1))
    gated_part(dpx(3, 0))
    gated_part(dpx(1, 0))
    wring[5].wait_recv()
    gated_part(dpx(3, 1))
    wring[6].wait_recv()
    gated_part(dpx(1, 1))
    wring[3].wait_recv()
    wring[7].start()
    wring[4].wait_recv()
    wring[8].start()
    gated_part(dpx(2, 0))
    wring[7].wait_recv()
    wring[8].wait_recv()
    gated_part(dpx(2, 1))

    def gate_rows(r, carry):
        part = pl.ds(pl.multiple_of(r * 16, 16), 16)
        values = att[part, :]
        center = values - jnp.mean(values, axis=-1, keepdims=True)
        inverse = lax.rsqrt(jnp.mean(center * center, axis=-1, keepdims=True) + NORM_EPS)
        nhat = center * inverse
        gate = jnp.concatenate([proj[m, part, pl.ds(COLS, COLS)] for m in range(DP)], axis=1).astype(F32)
        scaled = gate * norm_gain[...]
        gated[part, :] = (nhat * scaled).astype(BF16)
        grad_hat = grad_gated[part, :] * scaled
        along = jnp.mean(grad_hat * nhat, axis=-1, keepdims=True)
        grad = inverse * (grad_hat - jnp.mean(grad_hat, axis=-1, keepdims=True) - nhat * along)
        grad_att[part, :] = grad.astype(BF16)
        return carry

    lax.fori_loop(0, TOK // 16, gate_rows, 0)

    def gq_copy(k):
        to = dpo(k)
        return remote(gq_out.at[to], gq_in.at[d], gq_s.at[k], gq_r.at[k], (h, to))

    def attend_back(m):
        for k in range(2):
            head = m * 2 + k
            lanes = pl.ds(pl.multiple_of(head * HEAD, HEAD), HEAD)
            value_new = proj[m, :, pl.ds(2 * COLS + k * HEAD, HEAD)]
            key_new = proj[m, :, pl.ds(3 * COLS + k * HEAD, HEAD)]
            grad = grad_att[:, lanes]
            total = jnp.zeros((TOK, HEAD), F32)
            parts = (
                (kv[0, :, lanes], kv[1, :, lanes], pl.ds(0, CACHED)),
                (key_new, value_new, pl.ds(CACHED, TOK)),
            )
            for keys, values, where in parts:
                grad_score = dot_nt(grad, values) * slope[head, :, where]
                tsum[head, :, where] = jnp.sum(grad_score.reshape(TOK // 8, 8, -1), axis=0)
                total = total + dot_nn(grad_score.astype(BF16), keys)
            gq_out[m, :, pl.ds(k * HEAD, HEAD)] = (total * SCALE).astype(BF16)

    def back_step(k, carry):
        attend_back(dpo(k))
        gq_copy(k).start()
        return carry

    lax.fori_loop(1, DP, back_step, 0)
    attend_back(d)
    gq_in[d] = gq_out[d]

    table = jnp.zeros((HEADS, BUCKETS), F32)
    for term in reversed(three_parts(jnp.sum(tsum[...], axis=1))):
        table = table + dot_nt(term, hot)
    tab_one[d] = table

    def t1_copy(k):
        return remote(tab_one.at[d], tab_one.at[d], t1_s.at[k], t1_r.at[k], (h, dpo(k)))

    def t2_copy(k):
        return remote(tab_two.at[h], tab_two.at[h], t2_s.at[k], t2_r.at[k], (hist(k), d))

    def run(copy, stop, what):
        def step(k, carry):
            one = copy(k)
            getattr(one, what)()
            return carry

        lax.fori_loop(1, stop, step, 0)

    run(t1_copy, DP, "start")
    run(gq_copy, DP, "wait_recv")

    for i in range(DP):
        grad_pre = (gq_in[i].astype(F32) * pre_slope[i]).astype(BF16)
        grad_pre_t[:, pl.ds(i * TOK, TOK)] = grad_pre.T

    def rs_copy(k):
        to = hist(k)
        return remote(rs_out.at[to], rs_in.at[h], rs_s.at[k], rs_r.at[k], (to, d))

    def slice_of(s):
        lanes = pl.ds(pl.multiple_of(s * TOK, TOK), TOK)
        return dot_nn(grad_pre_t[...], rows[:, :, lanes].reshape(DP * TOK, TOK))

    def rs_step(k, carry):
        to = hist(k)
        rs_out[to] = slice_of(to).astype(BF16)
        rs_copy(k).start()
        return carry

    lax.fori_loop(1, HIST, rs_step, 0)
    own_slice = slice_of(h)

    run(t1_copy, DP, "wait_recv")
    table = tab_one[0]
    for i in range(1, DP):
        table = table + tab_one[i]
    tab_two[h] = table
    run(t2_copy, HIST, "start")

    def out_cols(m, carry):
        lanes = pl.ds(pl.multiple_of(m * COLS, COLS), COLS)
        out_ref[:, lanes] = (dot_nn(gated[...], wout[m]) + act[:, lanes].astype(F32)).astype(BF16)
        return carry

    lax.fori_loop(0, DP, out_cols, 0)

    rs_in[h] = jnp.zeros((COLS, TOK), BF16)
    run(rs_copy, HIST, "wait_recv")
    total = own_slice
    for i in range(HIST):
        total = total + rs_in[i].astype(F32)
    ag_out[...] = total.T.astype(BF16)

    own_rows = gsum_hbm.at[pl.ds(pl.multiple_of(h * TOK, TOK), TOK), :]

    def ag_copy(k):
        return remote(ag_out, own_rows, ag_s.at[k], ag_r.at[k], (hist(k), d))

    run(ag_copy, HIST, "start")
    own_gsum = pltpu.make_async_copy(ag_out, own_rows, loc_sem.at[8])
    own_gsum.start()

    run(t2_copy, HIST, "wait_recv")
    table = tab_two[0]
    for i in range(1, HIST):
        table = table + tab_two[i]
    gtab_ref[...] = table

    for copy in ring + wring:
        copy.wait_send()
    for copy, stop in ((kv_copy, HIST), (bk_copy, HIST), (pj_copy, DP), (gq_copy, DP), (rs_copy, HIST), (t1_copy, DP), (t2_copy, HIST)):
        run(copy, stop, "wait_send")
    run(ag_copy, HIST, "wait_recv")
    run(ag_copy, HIST, "wait_send")
    own_gsum.wait()


def layer(actions, cotangent, cache, length, buckets, new_bucket, ln_gain, norm_gain, w_frozen, w_query, w_out, rab):
    any_space = pl.BlockSpec(memory_space=pl.ANY)
    vmem = pl.BlockSpec(memory_space=pltpu.VMEM)
    smem = pl.BlockSpec(memory_space=pltpu.SMEM)
    dma = pltpu.SemaphoreType.DMA
    sem_sizes = (9, HIST, HIST, HIST, HIST, 9, 9, DP, DP, 9, 9, DP, DP, HIST, HIST, HIST, HIST, DP, DP, HIST, HIST)
    return pl.pallas_call(
        kernel,
        out_shape=(
            jax.ShapeDtypeStruct((TOK, WIDTH), BF16),
            jax.ShapeDtypeStruct((WIDTH, COLS), BF16),
            jax.ShapeDtypeStruct((HEADS, BUCKETS), F32),
        ),
        in_specs=[any_space, any_space, any_space, smem, any_space, vmem, vmem, vmem, any_space, any_space, any_space, vmem],
        out_specs=(vmem, any_space, vmem),
        scratch_shapes=[
            pltpu.VMEM((TOK, WIDTH), BF16),
            pltpu.VMEM((TOK, WIDTH), BF16),
            pltpu.VMEM((4, WIDTH, COLS), BF16),
            pltpu.VMEM((DP, TOK, WIDTH), BF16),
            pltpu.VMEM((DP, TOK, COLS), F32),
            pltpu.VMEM((DP, TOK, 4 * COLS), BF16),
            pltpu.VMEM((DP, TOK, 4 * COLS), BF16),
            pltpu.VMEM((2, CACHED, WIDTH), BF16),
            pltpu.VMEM((HIST, 8, TOK), jnp.int32),
            pltpu.VMEM((BUCKETS, KEYS), BF16),
            pltpu.VMEM((HEADS, KEYS), F32),
            pltpu.VMEM((TOK, WIDTH), F32),
            pltpu.VMEM((HEADS, TOK, KEYS), F32),
            pltpu.VMEM((DP, WIDTH, COLS), BF16),
            pltpu.VMEM((TOK, WIDTH), F32),
            pltpu.VMEM((TOK, WIDTH), BF16),
            pltpu.VMEM((TOK, WIDTH), BF16),
            pltpu.VMEM((HEADS, 8, KEYS), F32),
            pltpu.VMEM((DP, TOK, COLS), BF16),
            pltpu.VMEM((DP, TOK, COLS), BF16),
            pltpu.VMEM((COLS, DP * TOK), BF16),
            pltpu.VMEM((HIST, COLS, TOK), BF16),
            pltpu.VMEM((HIST, COLS, TOK), BF16),
            pltpu.VMEM((TOK, COLS), BF16),
            pltpu.VMEM((DP, HEADS, BUCKETS), F32),
            pltpu.VMEM((HIST, HEADS, BUCKETS), F32),
        ]
        + [dma((n,)) for n in sem_sizes],
        compiler_params=pltpu.CompilerParams(collective_id=0, has_side_effects=True, vmem_limit_bytes=60 * 1024 * 1024),
        name="layer",
    )(actions, cotangent, cache, length, buckets, new_bucket, ln_gain, norm_gain, w_frozen, w_query, w_out, rab)


def shards(
    actions, cotangent, cache_kv, cache_len, cache_bucket, new_bucket, ln_gain, norm_gain,
    w_frozen, w_query, query_m, query_v, w_out, rab_table, rab_m, rab_v,
):
    lane = lax.broadcasted_iota(jnp.int32, (HIST, 8, 4 * SLAB), 2)
    mine = lane // SLAB == lax.axis_index("history") % 4
    tiled = jnp.tile(cache_bucket.reshape(HIST, 1, SLAB), (1, 8, 4))
    buckets = jnp.where(mine, tiled, 0)
    result, grad_sum, grad_table = layer(
        actions.reshape(TOK, WIDTH),
        cotangent.reshape(TOK, WIDTH),
        cache_kv.reshape(2, HIST, SLAB, WIDTH),
        cache_len.reshape(1, 1),
        buckets,
        new_bucket.reshape(1, TOK),
        ln_gain.reshape(1, WIDTH),
        norm_gain.reshape(1, WIDTH),
        w_frozen,
        w_query,
        w_out,
        rab_table,
    )
    query_new, query_m_new, query_v_new = adam_update(w_query, query_m, query_v, grad_sum.astype(F32))
    rab_new, rab_m_new, rab_v_new = adam_update(rab_table, rab_m, rab_v, grad_table)
    return (result.reshape(actions.shape), query_new, query_m_new, query_v_new, rab_new, rab_m_new, rab_v_new)


def solution(mesh):
    placed = (
        P("history", "dp", None, None),
        P("history", "dp", None, None),
        P(None, None, "dp", "history", None),
        P("history", "dp"),
        P(None, "dp", "history"),
        P("history", "dp", None),
        P(),
        P(),
        P(None, None, "dp"),
        P(None, "dp"),
        P(None, "dp"),
        P(None, "dp"),
        P(None, "dp"),
        P(),
        P(),
        P(),
    )
    return jax.shard_map(
        shards,
        mesh=mesh,
        in_specs=placed,
        out_specs=(
            P("history", "dp", None, None),
            P(None, "dp"),
            P(None, "dp"),
            P(None, "dp"),
            P(),
            P(),
            P(),
        ),
        check_vma=False,
    )
```

time: 333 us -> 155 us (0.47)
  Pallas kernels: 0 us -> 144 us
  blocking collectives: 106 us -> 0 us
  waiting for transfers between devices: 89 us -> 0 us
  matrix products: 43.4 us -> 0 us
  local copies, waits for them, and re-layouts: 38.6 us -> 1.62 us
  starting transfers between devices: 17.4 us -> 0 us
  other arithmetic: 21.8 us -> 6.42 us
  between operations: 14.7 us -> 1.4 us
    pallas_call x0 -> x1, Pallas kernels: none -> 144 us  [layer(): pl.pallas_call(kernel, out_shape=(jax.ShapeDtypeStruct((TOK, WIDTH), BF16...]
    psum x1 -> x0, blocking collectives: 66 us -> none  [shards(): grad_table = lax.psum(grad_table, ('history', 'dp'))]
    all_to_all x3 -> x0, waiting for transfers between devices: 57.9 us -> none  [the longest x1 36.3 us: shards(): lax.all_to_all(cache_kv, 'history', split_axis=1, concat_axis=3, tiled=True)]
    dot_general x25 -> x0, matrix products: 43.4 us -> none  [the longest x3 7.57 us: forward_part(): jnp.einsum('htk,khd->thd', weights, values_part, preferred_element_type=j...]
    all_to_all x1 -> x0, blocking collectives: 39.6 us -> none  [shards(): lax.all_to_all(grad_query, 'dp', split_axis=1, concat_axis=0, tiled=True)]
    all_to_all x3 -> x0, starting transfers between devices: 17.1 us -> none  [the longest x1 8.14 us: shards(): lax.all_to_all(bucket_shard, 'history', split_axis=1, concat_axis=3, tile...]
    psum x1 -> x0, waiting for transfers between devices: 16.6 us -> none  [shards(): grad_sum = lax.psum(grad_weight, 'history')]
    all_gather x2 -> x0, waiting for transfers between devices: 13.8 us -> none  [the longest x1 13.7 us: shards(): group_rows = lax.all_gather(normed, 'dp', axis=0, tiled=True)]
  transfers between devices with their start and end apart: 6 -> 0, of which waited for: 5 -> 0; matrix products, arithmetic and copies ran while one was open for 18% -> 0% of each run, Pallas kernels for 0% -> 0%
where the time goes in v1:
time: 155 us; the launch traced here: 153 us
  Pallas kernels  144 us (93%)
  other arithmetic  6.42 us (4%)
  local copies, waits for them, and re-layouts  1.62 us (1%)
    pallas_call x1, Pallas kernels, layer(): pl.pallas_call(kernel, out_shape=(jax.ShapeDtypeStruct((TOK, WIDTH), BF16...  144 us
    convert_element_type x1, other arithmetic, adam_update(): return (stepped.astype(weight.dtype), first_new, second_new)  5.14 us

profile of v1, /device:TPU:0, one launch (start us, length us, event | category | flops | bytes accessed | tf_op | source)
XLA Modules:
  0.0 153.1 jit_solution(1196948787134528879)
XLA Ops:
  0.7 0.7 tile.14
  1.4 0.1 tile.15
  1.5 0.6 fusion.2.bucket_hbm
  2.7 0.0 copy-start
  2.8 0.0 copy-start.1
  2.8 143.6 %layer.1 = (bf16[128,2048]{1,0:T(8,128)(2,1)}, bf16[2048,256]{1,0:T(8,128)(2,1)}, f32[16,128]{1,0:T(8,128)}) custom-call(bf16[128,2048]{1,0:T(8,128)(2,1)} %bitcast.9, bf16[128,2048]{1,0:T(8,128)(2,1)} %bitcast.10, bf16[2,16,32,2048]{3,2,1,0:T(8,128)(2,1)} %bitcast.8, s32[1,1]{1,0:T(1,128)S(6)} %copy.24.length, s32[16,8,128]{2,1,0:T(8,128)} %fusion.2.bucket_hbm, ...), custom_call_target="tpu_custom_call" | custom-call | tf_op jit(solution)/shard_map/layer/pallas_call | solution.py:456
  146.4 0.0 copy-done
  146.4 0.0 copy-done.1
  146.4 0.0 copy-start.3
  146.5 0.0 copy-start.4
  146.5 0.0 copy-start.5
  146.5 0.0 copy-start.6
  146.5 0.0 copy-start.2
  146.5 5.1 %subtract_convert_fusion = (bf16[2048,256]{1,0:T(8,128)(2,1)}, f32[2048,256]{1,0:T(8,128)}, f32[2048,256]{1,0:T(8,128)}) fusion(bf16[2048,256]{1,0:T(8,128)(2,1)S(1)} %copy-done, bf16[2048,256]{1,0:T(8,128)(2,1)} %get-tuple-element.11, f32[2048,256]{1,0:T(8,128)S(1)} %copy-done.1, f32[2048,256]{1,0:T(8,128)} %param.27), kind=kLoop, calls=%fused_computation.4 | loop fusion | flops 7340032 | bytes 11534336 | tf_op jit(solution)/shard_map/convert_element_type | solution.py:38
  151.6 0.0 copy-done.3
  151.6 0.0 copy-done.4
  151.6 0.0 copy-done.5
  151.7 0.0 copy-done.6
  151.7 0.6 divide_subtract_fusion
  152.3 0.0 copy-done.2
  152.3 0.8 copy.25
  (2 shorter events, 0.0 us)
Async XLA Ops:
  2.7 143.7 %copy-start = (bf16[2048,256]{1,0:T(8,128)(2,1)S(1)}, bf16[2048,256]{1,0:T(8,128)(2,1)}, u32[]{:S(2)}) copy-start(bf16[2048,256]{1,0:T(8,128)(2,1)} %query_hbm.1) | copy-start | bytes 3145732
  2.8 143.7 %copy-start.1 = (f32[2048,256]{1,0:T(8,128)S(1)}, f32[2048,256]{1,0:T(8,128)}, u32[]{:S(2)}) copy-start(f32[2048,256]{1,0:T(8,128)} %param.26) | copy-start | bytes 6291460
  146.4 5.2 %copy-start.3 = (f32[16,128]{1,0:T(8,128)S(1)}, f32[16,128]{1,0:T(8,128)}, u32[]{:S(2)}) copy-start(f32[16,128]{1,0:T(8,128)} %rab.1) | copy-start | bytes 24580
  146.5 5.2 %copy-start.4 = (f32[16,128]{1,0:T(8,128)S(1)}, f32[16,128]{1,0:T(8,128)}, u32[]{:S(2)}) copy-start(f32[16,128]{1,0:T(8,128)} %param.30) | copy-start | bytes 24580
  146.5 5.2 %copy-start.5 = (f32[16,128]{1,0:T(8,128)S(1)}, f32[16,128]{1,0:T(8,128)}, u32[]{:S(2)}) copy-start(f32[16,128]{1,0:T(8,128)} %param.31) | copy-start | bytes 24580
  146.5 5.2 %copy-start.6 = (f32[16,128]{1,0:T(8,128)S(1)}, f32[16,128]{1,0:T(8,128)}, u32[]{:S(2)}) copy-start(f32[16,128]{1,0:T(8,128)} %get-tuple-element.12) | copy-start | bytes 24580
  146.5 5.8 %copy-start.2 = (bf16[128,2048]{1,0:T(8,128)(2,1)S(1)}, bf16[128,2048]{1,0:T(8,128)(2,1)}, u32[]{:S(2)}) copy-start(bf16[128,2048]{1,0:T(8,128)(2,1)} %get-tuple-element.10) | copy-start | bytes 1572868

commit v2 on v1

--- a/solution.py
+++ b/solution.py
@@ -29,6 +29,9 @@
 CACHED = HIST * SLAB
 KEYS = CACHED + TOK
 SCALE = HEAD ** (-0.5)
+KV_COPIES = 4 * (HIST - 1) + 1
+KV_HALF = 2 * (HIST - 1) + 1
+LINK_ORDER = (1, 4, 3, 12, 2, 8, 5, 15, 7, 13, 6, 9, 14, 11, 10)
 
 
 def adam_update(weight, moment_one, moment_two, gradient):
@@ -60,11 +63,11 @@
 
 
 def kernel(
-    act_hbm, cot_hbm, cache_hbm, length, bucket_hbm, new_bucket, ln_gain, norm_gain, frozen_hbm, query_hbm, wout_hbm, rab,
+    act_hbm, cot_hbm, cache_hbm, length, buckets, new_bucket, ln_gain, norm_gain, frozen_hbm, query_hbm, wout_hbm, rab,
     out_ref, gsum_hbm, gtab_ref,
-    act, cot, wts, rows, pre_slope, sent, proj, kv, bks, onehot, bias, att, slope, wout, grad_gated, gated, grad_att,
+    act, cot, wts, rows, pre_slope, sent, proj, kv, bk_out, bks, onehot, bias, att, slope, wout, grad_gated, gated, grad_att,
     tsum, gq_out, gq_in, grad_pre_t, rs_out, rs_in, ag_out, tab_one, tab_two,
-    loc_sem, kv_s, kv_r, bk_s, bk_r, g_s, g_r, pj_s, pj_r, w_s, w_r, gq_s, gq_r, rs_s, rs_r, ag_s, ag_r, t1_s, t1_r, t2_s, t2_r,
+    loc_sem, kv_s, kv_r, bk_s, bk_r, g_s, g_r, pj_s, pj_r, w_s, w_r, px_s, px_r, p1_s, p1_r, p2_s, p2_r, p3_s, p3_r, gq_s, gq_r, rs_s, rs_r, ag_s, ag_r, t1_s, t1_r, t2_s, t2_r,
 ):
     h = lax.axis_index("history")
     d = lax.axis_index("dp")
@@ -106,8 +109,10 @@
     own_slab = kv.at[:, pl.ds(pl.multiple_of(h * SLAB, SLAB), SLAB), :]
     load_kv = pltpu.make_async_copy(cache_hbm.at[:, h], own_slab, loc_sem.at[5])
     load_kv.start()
-    load_bk = pltpu.make_async_copy(bucket_hbm.at[h], bks.at[h], loc_sem.at[6])
-    load_bk.start()
+    lane = lax.broadcasted_iota(jnp.int32, (HIST, TOK), 1)
+    placed = jnp.where(lane // SLAB == y, jnp.concatenate([buckets[:, 0, :]] * 4, axis=1), 0)
+    for u in range(HIST):
+        bk_out[u] = jnp.broadcast_to(placed[u : u + 1, :], (8, TOK))
 
     load_act.wait()
 
@@ -127,41 +132,90 @@
             src_ref=src, dst_ref=dst, send_sem=send, recv_sem=recv, device_id=device, device_id_type=MESH
         )
 
-    def ring_gather(buffer, half_rows, own, send, recv):
+    def ring_gather(block, half, own, send, recv, first=0):
         right, left, sibling = (h, dpx(1, 0)), (h, dpx(3, 0)), (h, dpx(0, 1))
-        low, high = pl.ds(0, half_rows), pl.ds(half_rows, half_rows)
         from_left, from_right, far = dpx(3, 0), dpx(1, 0), dpx(2, 0)
         specs = [
-            (own, buffer.at[d], sibling),
-            (own, buffer.at[d], right),
-            (own, buffer.at[d], left),
-            (buffer.at[from_left, low], buffer.at[from_left, low], right),
-            (buffer.at[from_right, high], buffer.at[from_right, high], left),
-            (buffer.at[from_left], buffer.at[from_left], sibling),
-            (buffer.at[from_right], buffer.at[from_right], sibling),
-            (buffer.at[far, low], buffer.at[far, low], sibling),
-            (buffer.at[far, high], buffer.at[far, high], sibling),
+            (own, block(d), sibling),
+            (own, block(d), right),
+            (own, block(d), left),
+            (half(from_left, 0), half(from_left, 0), right),
+            (half(from_right, 1), half(from_right, 1), left),
+            (block(from_left), block(from_left), sibling),
+            (block(from_right), block(from_right), sibling),
+            (half(far, 0), half(far, 0), sibling),
+            (half(far, 1), half(far, 1), sibling),
         ]
-        return [remote(s, t, send.at[i], recv.at[i], dev) for i, (s, t, dev) in enumerate(specs)]
-
-    ring = ring_gather(rows, TOK // 2, rows.at[d], g_s, g_r)
+        numbered = list(enumerate(specs))[first:]
+        return {i: remote(s, t, send.at[i], recv.at[i], dev) for i, (s, t, dev) in numbered}
+
+    ring = ring_gather(
+        lambda i: rows.at[i],
+        lambda i, k: rows.at[i, pl.ds(k * (TOK // 2), TOK // 2)],
+        rows.at[d],
+        g_s,
+        g_r,
+    )
     for i in (1, 2, 0):
         ring[i].start()
 
-    def kv_copy(k):
-        to = hist(k)
-        return remote(cache_hbm.at[:, to], own_slab, kv_s.at[k], kv_r.at[k], (to, d))
+    def kv_copy(i):
+        piece, turn = divmod(i - 1, HIST - 1)
+        to = hist(LINK_ORDER[turn])
+        part, low = piece % 2, piece // 2 * 16
+        src = cache_hbm.at[part, to, pl.ds(low, 16)]
+        dst = kv.at[part, pl.ds(pl.multiple_of(h * SLAB + low, 16), 16), :]
+        return remote(src, dst, kv_s.at[i], kv_r.at[i], (to, d))
 
     def bk_copy(k):
         to = hist(k)
-        return remote(bucket_hbm.at[to], bks.at[h], bk_s.at[k], bk_r.at[k], (to, d))
-
-    def send_cache(k, carry):
+        return remote(bk_out.at[to], bks.at[h], bk_s.at[k], bk_r.at[k], (to, d))
+
+    def plane_x(k):
+        return remote(wout_hbm.at[0, z, y], wout.at[d, 0, z, y], px_s.at[k], px_r.at[k], (h, dpx(k, 0)))
+
+    def plane_one(k, kx):
+        slot, i = dpx(kx, 0), 3 * (k - 1) + kx - 1
+        over_z, over_y = wout.at[slot, 0, z, y, 0], wout.at[slot, 0, z, y, 1]
+        to_z, to_y = lax.rem(z + k, 4) * 4 + y, z * 4 + lax.rem(y + k, 4)
+        return (
+            remote(over_z, over_z, p1_s.at[i], p1_r.at[i], (to_z, d)),
+            remote(over_y, over_y, p1_s.at[9 + i], p1_r.at[9 + i], (to_y, d)),
+        )
+
+    def plane_two(k, kx):
+        slot, i = dpx(kx, 0), 3 * (k - 1) + kx - 1
+        over_y, over_z = wout.at[slot, 0, :, y, 0], wout.at[slot, 0, z, :, 1]
+        to_z, to_y = lax.rem(z + k, 4) * 4 + y, z * 4 + lax.rem(y + k, 4)
+        return (
+            remote(over_y, over_y, p2_s.at[i], p2_r.at[i], (to_y, d)),
+            remote(over_z, over_z, p2_s.at[9 + i], p2_r.at[9 + i], (to_z, d)),
+        )
+
+    def plane_share(kx):
+        block = wout.at[dpx(kx, 0), 0]
+        return remote(block, block, p3_s.at[kx], p3_r.at[kx], (h, dpx(0, 1)))
+
+    own_wout = remote(wout_hbm, wout.at[d], p3_s.at[0], p3_r.at[0], (h, dpx(0, 1)))
+    wring = ring_gather(
+        lambda i: wout.at[i, 1],
+        lambda i, k: wout.at[i, 1, pl.ds(2 * k, 2)],
+        wout_hbm.at[1],
+        w_s,
+        w_r,
+        first=1,
+    )
+    plane_steps = [(k, kx) for k in (1, 3, 2) for kx in (1, 2, 3)]
+    for k in range(1, 4):
+        plane_x(k).start()
+
+    def send_bk(k, carry):
         bk_copy(k).start()
-        kv_copy(k).start()
-        return carry
-
-    lax.fori_loop(1, HIST, send_cache, 0)
+        return carry
+
+    lax.fori_loop(1, HIST, send_bk, 0)
+    for i in range(1, KV_HALF):
+        kv_copy(i).start()
 
     def project(chip):
         part = pl.ds(pl.multiple_of(chip * 2, 2), 2)
@@ -185,6 +239,13 @@
     pj_copy(1).start()
     own_proj = pltpu.make_async_copy(sent.at[d], proj.at[d], loc_sem.at[7])
     own_proj.start()
+    for k in range(1, 4):
+        plane_x(k).wait_recv()
+    for step in plane_steps:
+        for copy in plane_one(*step):
+            copy.start()
+    for i in range(KV_HALF, KV_COPIES):
+        kv_copy(i).start()
     ring[1].wait_recv()
     ring[3].start()
     ring[5].start()
@@ -199,6 +260,9 @@
     project(lax.rem(x + 1, 4))
     pj_copy(2).start()
     pj_copy(3).start()
+    for i in (1, 2):
+        wring[i].start()
+    own_wout.start()
     ring[3].wait_recv()
     ring[7].start()
     ring[4].wait_recv()
@@ -209,11 +273,14 @@
     pj_copy(4).start()
     pj_copy(5).start()
 
-    wring = ring_gather(wout, WIDTH // 2, wout_hbm, w_s, w_r)
-    for i in (1, 2, 0):
-        wring[i].start()
-
-    load_bk.wait()
+    for step in plane_steps:
+        for copy in plane_one(*step):
+            copy.wait_recv()
+    for step in plane_steps:
+        for copy in plane_two(*step):
+            copy.start()
+
+    bks[h] = bk_out[h]
 
     def wait_bk(k, carry):
         bk_copy(k).wait_recv()
@@ -239,6 +306,11 @@
     col_pos = lax.broadcasted_iota(jnp.int32, (TOK, TOK), 1)
     share_new = jnp.where(col_pos <= row_pos, jnp.broadcast_to(share, (TOK, TOK)), 0.0)
 
+    for i in (1, 2):
+        wring[i].wait_recv()
+        wring[i + 2].start()
+        wring[i + 4].start()
+
     def wait_pj(k, carry):
         pj_copy(k).wait_recv()
         return carry
@@ -246,12 +318,9 @@
     own_proj.wait()
     lax.fori_loop(1, DP, wait_pj, 0)
 
-    def wait_kv(k, carry):
-        kv_copy(k).wait_recv()
-        return carry
-
     load_kv.wait()
-    lax.fori_loop(1, HIST, wait_kv, 0)
+    for i in range(1, KV_COPIES):
+        kv_copy(i).wait_recv()
 
     def attend(m, carry):
         for k in range(2):
@@ -275,41 +344,47 @@
             att[:, lanes] = total
         return carry
 
-    lax.fori_loop(0, DP, attend, 0)
+    lax.fori_loop(0, DP // 2, attend, 0)
+    for step in plane_steps:
+        for copy in plane_two(*step):
+            copy.wait_recv()
+    for k in range(1, 4):
+        plane_share(k).start()
+    for i in (3, 4):
+        wring[i].wait_recv()
+        wring[i + 4].start()
+    lax.fori_loop(DP // 2, DP, attend, 0)
 
     load_cot.wait()
     load_wout.wait()
 
-    def gated_part(m, first=False):
+    def gated_part(m, half, first=False):
         lanes = pl.ds(pl.multiple_of(m * COLS, COLS), COLS)
-        for n in range(4):
-            cols = pl.ds(n * 512, 512)
-            part = dot_nt(cot[:, lanes], wout[m, cols, :])
+        for n in range(2):
+            cols = pl.ds(half * 1024 + n * 512, 512)
+            part = dot_nt(cot[:, lanes], wout[m, half, pl.ds(2 * n, 2)].reshape(512, COLS))
             grad_gated[:, cols] = part if first else grad_gated[:, cols] + part
 
-    gated_part(d, True)
-    wring[1].wait_recv()
-    wring[3].start()
-    wring[5].start()
-    wring[2].wait_recv()
-    wring[4].start()
-    wring[6].start()
-    wring[0].wait_recv()
-    gated_part(dpx(0, 1))
-    gated_part(dpx(3, 0))
-    gated_part(dpx(1, 0))
+    gated_part(d, 0, True)
+    gated_part(d, 1, True)
+    own_wout.wait_recv()
+    gated_part(dpx(0, 1), 0)
+    gated_part(dpx(0, 1), 1)
+    for k in (3, 1, 2):
+        gated_part(dpx(k, 0), 0)
+    for k in (3, 1, 2):
+        plane_share(k).wait_recv()
+        gated_part(dpx(k, 1), 0)
+    gated_part(dpx(3, 0), 1)
+    gated_part(dpx(1, 0), 1)
     wring[5].wait_recv()
-    gated_part(dpx(3, 1))
+    gated_part(dpx(3, 1), 1)
     wring[6].wait_recv()
-    gated_part(dpx(1, 1))
-    wring[3].wait_recv()
-    wring[7].start()
-    wring[4].wait_recv()
-    wring[8].start()
-    gated_part(dpx(2, 0))
+    gated_part(dpx(1, 1), 1)
+    gated_part(dpx(2, 0), 1)
     wring[7].wait_recv()
     wring[8].wait_recv()
-    gated_part(dpx(2, 1))
+    gated_part(dpx(2, 1), 1)
 
     def gate_rows(r, carry):
         part = pl.ds(pl.multiple_of(r * 16, 16), 16)
@@ -328,79 +403,113 @@
 
     lax.fori_loop(0, TOK // 16, gate_rows, 0)
 
-    def gq_copy(k):
-        to = dpo(k)
-        return remote(gq_out.at[to], gq_in.at[d], gq_s.at[k], gq_r.at[k], (h, to))
-
-    def attend_back(m):
-        for k in range(2):
-            head = m * 2 + k
-            lanes = pl.ds(pl.multiple_of(head * HEAD, HEAD), HEAD)
-            value_new = proj[m, :, pl.ds(2 * COLS + k * HEAD, HEAD)]
-            key_new = proj[m, :, pl.ds(3 * COLS + k * HEAD, HEAD)]
-            grad = grad_att[:, lanes]
-            total = jnp.zeros((TOK, HEAD), F32)
-            parts = (
-                (kv[0, :, lanes], kv[1, :, lanes], pl.ds(0, CACHED)),
-                (key_new, value_new, pl.ds(CACHED, TOK)),
-            )
-            for keys, values, where in parts:
-                grad_score = dot_nt(grad, values) * slope[head, :, where]
-                tsum[head, :, where] = jnp.sum(grad_score.reshape(TOK // 8, 8, -1), axis=0)
-                total = total + dot_nn(grad_score.astype(BF16), keys)
-            gq_out[m, :, pl.ds(k * HEAD, HEAD)] = (total * SCALE).astype(BF16)
-
-    def back_step(k, carry):
-        attend_back(dpo(k))
-        gq_copy(k).start()
-        return carry
-
-    lax.fori_loop(1, DP, back_step, 0)
-    attend_back(d)
-    gq_in[d] = gq_out[d]
+    def gq_copy(half, k):
+        to, i = dpo(k), half * DP + k
+        return remote(gq_out.at[half, to], gq_in.at[half, d], gq_s.at[i], gq_r.at[i], (h, to))
+
+    def attend_back(m, k):
+        head = m * 2 + k
+        lanes = pl.ds(pl.multiple_of(head * HEAD, HEAD), HEAD)
+        value_new = proj[m, :, pl.ds(2 * COLS + k * HEAD, HEAD)]
+        key_new = proj[m, :, pl.ds(3 * COLS + k * HEAD, HEAD)]
+        grad = grad_att[:, lanes]
+        total = jnp.zeros((TOK, HEAD), F32)
+        parts = (
+            (kv[0, :, lanes], kv[1, :, lanes], pl.ds(0, CACHED)),
+            (key_new, value_new, pl.ds(CACHED, TOK)),
+        )
+        for keys, values, where in parts:
+            grad_score = dot_nt(grad, values) * slope[head, :, where]
+            tsum[head, :, where] = jnp.sum(grad_score.reshape(TOK // 8, 8, -1), axis=0)
+            total = total + dot_nn(grad_score.astype(BF16), keys)
+        gq_out[k, m] = (total * SCALE).astype(BF16)
+
+    def back_steps(half, first, stop):
+        def step(k, carry):
+            attend_back(dpo(k), half)
+            gq_copy(half, k).start()
+            return carry
+
+        lax.fori_loop(first, stop, step, 0)
+
+    def run(copy, stop, what, *half):
+        def step(k, carry):
+            getattr(copy(*half, k), what)()
+            return carry
+
+        lax.fori_loop(1, stop, step, 0)
+
+    def own_back(half):
+        attend_back(d, half)
+        gq_in[half, d] = gq_out[half, d]
+
+    def rs_copy(half, k):
+        to, i = hist(k), half * HIST + k
+        return remote(rs_out.at[half, to], rs_in.at[half, h], rs_s.at[i], rs_r.at[i], (to, d))
+
+    def weight_half(half):
+        run(gq_copy, DP, "wait_recv", half)
+        for i in range(DP):
+            pre = pre_slope[i, :, pl.ds(half * HEAD, HEAD)]
+            grad_pre_t[half, :, pl.ds(i * TOK, TOK)] = (gq_in[half, i].astype(F32) * pre).astype(BF16).T
+        for kz in (1, 3, 2, 0):
+            to_z = lax.rem(z + kz, 4)
+            lanes = pl.ds(pl.multiple_of(to_z * 512, 512), 512)
+            piece = dot_nn(grad_pre_t[half], rows[:, :, lanes].reshape(DP * TOK, 512)).astype(BF16)
+            for j in range(4):
+                rs_out[half, to_z * 4 + j] = piece[:, j * TOK : (j + 1) * TOK]
+            for ky in (1, 0, 3, 2):
+                if kz or ky:
+                    rs_copy(half, kz * 4 + ky).start()
+        rs_in[half, h] = rs_out[half, h]
+
+    def ag_copy(half, k):
+        block = gsum_hbm.at[pl.ds(pl.multiple_of(h * TOK, TOK), TOK), pl.ds(half * HEAD, HEAD)]
+        i = half * HIST + k
+        return remote(ag_out.at[half], block, ag_s.at[i], ag_r.at[i], (hist(k), d))
+
+    def own_gsum(half):
+        block = gsum_hbm.at[pl.ds(pl.multiple_of(h * TOK, TOK), TOK), pl.ds(half * HEAD, HEAD)]
+        return pltpu.make_async_copy(ag_out.at[half], block, loc_sem.at[8 + half])
+
+    def gather_half(half):
+        run(rs_copy, HIST, "wait_recv", half)
+        total = rs_in[half, 0].astype(F32)
+        for i in range(1, HIST):
+            total = total + rs_in[half, i].astype(F32)
+        ag_out[half] = total.T.astype(BF16)
+        for k in LINK_ORDER:
+            ag_copy(half, k).start()
+        own_gsum(half).start()
+
+    def out_cols(m, carry):
+        lanes = pl.ds(pl.multiple_of(m * COLS, COLS), COLS)
+        product = dot_nn(gated[...], wout[m].reshape(WIDTH, COLS))
+        out_ref[:, lanes] = (product + act[:, lanes].astype(F32)).astype(BF16)
+        return carry
+
+    def t1_copy(k):
+        return remote(tab_one.at[d], tab_one.at[d], t1_s.at[k], t1_r.at[k], (h, dpo(k)))
+
+    def t2_copy(k):
+        return remote(tab_two.at[h], tab_two.at[h], t2_s.at[k], t2_r.at[k], (hist(k), d))
+
+    back_steps(0, 1, DP)
+    own_back(0)
+    back_steps(1, 1, 4)
+    weight_half(0)
+    back_steps(1, 4, DP)
+    own_back(1)
 
     table = jnp.zeros((HEADS, BUCKETS), F32)
     for term in reversed(three_parts(jnp.sum(tsum[...], axis=1))):
         table = table + dot_nt(term, hot)
     tab_one[d] = table
-
-    def t1_copy(k):
-        return remote(tab_one.at[d], tab_one.at[d], t1_s.at[k], t1_r.at[k], (h, dpo(k)))
-
-    def t2_copy(k):
-        return remote(tab_two.at[h], tab_two.at[h], t2_s.at[k], t2_r.at[k], (hist(k), d))
-
-    def run(copy, stop, what):
-        def step(k, carry):
-            one = copy(k)
-            getattr(one, what)()
-            return carry
-
-        lax.fori_loop(1, stop, step, 0)
-
     run(t1_copy, DP, "start")
-    run(gq_copy, DP, "wait_recv")
-
-    for i in range(DP):
-        grad_pre = (gq_in[i].astype(F32) * pre_slope[i]).astype(BF16)
-        grad_pre_t[:, pl.ds(i * TOK, TOK)] = grad_pre.T
-
-    def rs_copy(k):
-        to = hist(k)
-        return remote(rs_out.at[to], rs_in.at[h], rs_s.at[k], rs_r.at[k], (to, d))
-
-    def slice_of(s):
-        lanes = pl.ds(pl.multiple_of(s * TOK, TOK), TOK)
-        return dot_nn(grad_pre_t[...], rows[:, :, lanes].reshape(DP * TOK, TOK))
-
-    def rs_step(k, carry):
-        to = hist(k)
-        rs_out[to] = slice_of(to).astype(BF16)
-        rs_copy(k).start()
-        return carry
-
-    lax.fori_loop(1, HIST, rs_step, 0)
-    own_slice = slice_of(h)
+
+    lax.fori_loop(0, DP // 2, out_cols, 0)
+    weight_half(1)
+    gather_half(0)
 
     run(t1_copy, DP, "wait_recv")
     table = tab_one[0]
@@ -409,28 +518,8 @@
     tab_two[h] = table
     run(t2_copy, HIST, "start")
 
-    def out_cols(m, carry):
-        lanes = pl.ds(pl.multiple_of(m * COLS, COLS), COLS)
-        out_ref[:, lanes] = (dot_nn(gated[...], wout[m]) + act[:, lanes].astype(F32)).astype(BF16)
-        return carry
-
-    lax.fori_loop(0, DP, out_cols, 0)
-
-    rs_in[h] = jnp.zeros((COLS, TOK), BF16)
-    run(rs_copy, HIST, "wait_recv")
-    total = own_slice
-    for i in range(HIST):
-        total = total + rs_in[i].astype(F32)
-    ag_out[...] = total.T.astype(BF16)
-
-    own_rows = gsum_hbm.at[pl.ds(pl.multiple_of(h * TOK, TOK), TOK), :]
-
-    def ag_copy(k):
-        return remote(ag_out, own_rows, ag_s.at[k], ag_r.at[k], (hist(k), d))
-
-    run(ag_copy, HIST, "start")
-    own_gsum = pltpu.make_async_copy(ag_out, own_rows, loc_sem.at[8])
-    own_gsum.start()
+    lax.fori_loop(DP // 2, DP, out_cols, 0)
+    gather_half(1)
 
     run(t2_copy, HIST, "wait_recv")
     table = tab_two[0]
@@ -438,13 +527,24 @@
         table = table + tab_two[i]
     gtab_ref[...] = table
 
-    for copy in ring + wring:
+    for copy in [*ring.values(), *wring.values(), own_wout]:
         copy.wait_send()
-    for copy, stop in ((kv_copy, HIST), (bk_copy, HIST), (pj_copy, DP), (gq_copy, DP), (rs_copy, HIST), (t1_copy, DP), (t2_copy, HIST)):
+    for k in range(1, 4):
+        plane_x(k).wait_send()
+        plane_share(k).wait_send()
+    for step in plane_steps:
+        for copy in plane_one(*step) + plane_two(*step):
+            copy.wait_send()
+    for i in range(1, KV_COPIES):
+        kv_copy(i).wait_send()
+    for copy, stop in ((bk_copy, HIST), (pj_copy, DP), (t1_copy, DP), (t2_copy, HIST)):
         run(copy, stop, "wait_send")
-    run(ag_copy, HIST, "wait_recv")
-    run(ag_copy, HIST, "wait_send")
-    own_gsum.wait()
+    for half in range(2):
+        run(gq_copy, DP, "wait_send", half)
+        run(rs_copy, HIST, "wait_send", half)
+        run(ag_copy, HIST, "wait_recv", half)
+        run(ag_copy, HIST, "wait_send", half)
+        own_gsum(half).wait()
 
 
 def layer(actions, cotangent, cache, length, buckets, new_bucket, ln_gain, norm_gain, w_frozen, w_query, w_out, rab):
@@ -452,7 +552,7 @@
     vmem = pl.BlockSpec(memory_space=pltpu.VMEM)
     smem = pl.BlockSpec(memory_space=pltpu.SMEM)
     dma = pltpu.SemaphoreType.DMA
-    sem_sizes = (9, HIST, HIST, HIST, HIST, 9, 9, DP, DP, 9, 9, DP, DP, HIST, HIST, HIST, HIST, DP, DP, HIST, HIST)
+    sem_sizes = (10, KV_COPIES, KV_COPIES, HIST, HIST, 9, 9, DP, DP, 9, 9, 4, 4, 18, 18, 18, 18, 4, 4, 2 * DP, 2 * DP, 2 * HIST, 2 * HIST, 2 * HIST, 2 * HIST, DP, DP, HIST, HIST)
     return pl.pallas_call(
         kernel,
         out_shape=(
@@ -460,7 +560,7 @@
             jax.ShapeDtypeStruct((WIDTH, COLS), BF16),
             jax.ShapeDtypeStruct((HEADS, BUCKETS), F32),
         ),
-        in_specs=[any_space, any_space, any_space, smem, any_space, vmem, vmem, vmem, any_space, any_space, any_space, vmem],
+        in_specs=[any_space, any_space, any_space, smem, vmem, vmem, vmem, vmem, any_space, any_space, any_space, vmem],
         out_specs=(vmem, any_space, vmem),
         scratch_shapes=[
             pltpu.VMEM((TOK, WIDTH), BF16),
@@ -472,21 +572,22 @@
             pltpu.VMEM((DP, TOK, 4 * COLS), BF16),
             pltpu.VMEM((2, CACHED, WIDTH), BF16),
             pltpu.VMEM((HIST, 8, TOK), jnp.int32),
+        pltpu.VMEM((HIST, 8, TOK), jnp.int32),
             pltpu.VMEM((BUCKETS, KEYS), BF16),
             pltpu.VMEM((HEADS, KEYS), F32),
             pltpu.VMEM((TOK, WIDTH), F32),
             pltpu.VMEM((HEADS, TOK, KEYS), F32),
-            pltpu.VMEM((DP, WIDTH, COLS), BF16),
+            pltpu.VMEM((DP, 2, 4, 4, 2, 32, COLS), BF16),
             pltpu.VMEM((TOK, WIDTH), F32),
             pltpu.VMEM((TOK, WIDTH), BF16),
             pltpu.VMEM((TOK, WIDTH), BF16),
             pltpu.VMEM((HEADS, 8, KEYS), F32),
-            pltpu.VMEM((DP, TOK, COLS), BF16),
-            pltpu.VMEM((DP, TOK, COLS), BF16),
-            pltpu.VMEM((COLS, DP * TOK), BF16),
-            pltpu.VMEM((HIST, COLS, TOK), BF16),
-            pltpu.VMEM((HIST, COLS, TOK), BF16),
-            pltpu.VMEM((TOK, COLS), BF16),
+            pltpu.VMEM((2, DP, TOK, HEAD), BF16),
+            pltpu.VMEM((2, DP, TOK, HEAD), BF16),
+            pltpu.VMEM((2, HEAD, DP * TOK), BF16),
+            pltpu.VMEM((2, HIST, HEAD, TOK), BF16),
+            pltpu.VMEM((2, HIST, HEAD, TOK), BF16),
+            pltpu.VMEM((2, TOK, HEAD), BF16),
             pltpu.VMEM((DP, HEADS, BUCKETS), F32),
             pltpu.VMEM((HIST, HEADS, BUCKETS), F32),
         ]
@@ -500,22 +601,18 @@
     actions, cotangent, cache_kv, cache_len, cache_bucket, new_bucket, ln_gain, norm_gain,
     w_frozen, w_query, query_m, query_v, w_out, rab_table, rab_m, rab_v,
 ):
-    lane = lax.broadcasted_iota(jnp.int32, (HIST, 8, 4 * SLAB), 2)
-    mine = lane // SLAB == lax.axis_index("history") % 4
-    tiled = jnp.tile(cache_bucket.reshape(HIST, 1, SLAB), (1, 8, 4))
-    buckets = jnp.where(mine, tiled, 0)
     result, grad_sum, grad_table = layer(
         actions.reshape(TOK, WIDTH),
         cotangent.reshape(TOK, WIDTH),
         cache_kv.reshape(2, HIST, SLAB, WIDTH),
         cache_len.reshape(1, 1),
-        buckets,
+        cache_bucket,
         new_bucket.reshape(1, TOK),
         ln_gain.reshape(1, WIDTH),
         norm_gain.reshape(1, WIDTH),
         w_frozen,
         w_query,
-        w_out,
+        w_out.reshape(2, 4, 4, 2, 32, COLS),
         rab_table,
     )
     query_new, query_m_new, query_v_new = adam_update(w_query, query_m, query_v, grad_sum.astype(F32))

time: 155 us -> 129 us (0.83)
  Pallas kernels: 144 us -> 120 us
    pallas_call x1, Pallas kernels: 144 us -> 120 us  [layer(): pl.pallas_call(kernel, out_shape=(jax.ShapeDtypeStruct((TOK, WIDTH), BF16...]
where the time goes in v2:
time: 129 us; the launch traced here: 128 us
  Pallas kernels  120 us (93%)
  other arithmetic  5.76 us (4%)
  between operations  1.38 us (1%)
    pallas_call x1, Pallas kernels, layer(): pl.pallas_call(kernel, out_shape=(jax.ShapeDtypeStruct((TOK, WIDTH), BF16...  120 us
    convert_element_type x1, other arithmetic, adam_update(): return (stepped.astype(weight.dtype), first_new, second_new)  5.14 us

profile of v2, /device:TPU:0, one launch (start us, length us, event | category | flops | bytes accessed | tf_op | source)
XLA Modules:
  0.0 128.1 jit_solution(10631471970378778925)
XLA Ops:
  1.3 0.0 copy-start
  1.3 0.0 copy-start.1
  1.3 120.1 %layer.1 = (bf16[128,2048]{1,0:T(8,128)(2,1)}, bf16[2048,256]{1,0:T(8,128)(2,1)}, f32[16,128]{1,0:T(8,128)}) custom-call(bf16[128,2048]{1,0:T(8,128)(2,1)} %bitcast.11, bf16[128,2048]{1,0:T(8,128)(2,1)} %bitcast.12, bf16[2,16,32,2048]{3,2,1,0:T(8,128)(2,1)} %bitcast.8, s32[1,1]{1,0:T(1,128)S(6)} %copy.24.length, s32[16,1,32]{2,1,0:T(1,128)} %buckets.1, ...), custom_call_target="tpu_custom_call" | custom-call | tf_op jit(solution)/shard_map/layer/pallas_call | solution.py:556
  121.4 0.0 copy-done
  121.5 0.0 copy-done.1
  121.5 0.0 copy-start.3
  121.5 0.0 copy-start.4
  121.5 0.0 copy-start.5
  121.5 0.0 copy-start.6
  121.5 0.0 copy-start.2
  121.5 5.1 %subtract_convert_fusion = (bf16[2048,256]{1,0:T(8,128)(2,1)}, f32[2048,256]{1,0:T(8,128)}, f32[2048,256]{1,0:T(8,128)}) fusion(bf16[2048,256]{1,0:T(8,128)(2,1)S(1)} %copy-done, bf16[2048,256]{1,0:T(8,128)(2,1)} %get-tuple-element.11, f32[2048,256]{1,0:T(8,128)S(1)} %copy-done.1, f32[2048,256]{1,0:T(8,128)} %param.27), kind=kLoop, calls=%fused_computation.4 | loop fusion | flops 7340032 | bytes 11534336 | tf_op jit(solution)/shard_map/convert_element_type | solution.py:41
  126.7 0.0 copy-done.3
  126.7 0.0 copy-done.4
  126.7 0.0 copy-done.5
  126.7 0.0 copy-done.6
  126.7 0.6 divide_subtract_fusion
  127.3 0.0 copy-done.2
  127.3 0.8 copy.25
Async XLA Ops:
  1.3 120.2 %copy-start = (bf16[2048,256]{1,0:T(8,128)(2,1)S(1)}, bf16[2048,256]{1,0:T(8,128)(2,1)}, u32[]{:S(2)}) copy-start(bf16[2048,256]{1,0:T(8,128)(2,1)} %query_hbm.1) | copy-start | bytes 3145732
  1.3 120.2 %copy-start.1 = (f32[2048,256]{1,0:T(8,128)S(1)}, f32[2048,256]{1,0:T(8,128)}, u32[]{:S(2)}) copy-start(f32[2048,256]{1,0:T(8,128)} %param.26) | copy-start | bytes 6291460
  121.5 5.2 %copy-start.3 = (f32[16,128]{1,0:T(8,128)S(1)}, f32[16,128]{1,0:T(8,128)}, u32[]{:S(2)}) copy-start(f32[16,128]{1,0:T(8,128)} %rab.1) | copy-start | bytes 24580
  121.5 5.2 %copy-start.4 = (f32[16,128]{1,0:T(8,128)S(1)}, f32[16,128]{1,0:T(8,128)}, u32[]{:S(2)}) copy-start(f32[16,128]{1,0:T(8,128)} %param.30) | copy-start | bytes 24580
  121.5 5.2 %copy-start.5 = (f32[16,128]{1,0:T(8,128)S(1)}, f32[16,128]{1,0:T(8,128)}, u32[]{:S(2)}) copy-start(f32[16,128]{1,0:T(8,128)} %param.31) | copy-start | bytes 24580
  121.5 5.2 %copy-start.6 = (f32[16,128]{1,0:T(8,128)S(1)}, f32[16,128]{1,0:T(8,128)}, u32[]{:S(2)}) copy-start(f32[16,128]{1,0:T(8,128)} %get-tuple-element.12) | copy-start | bytes 24580
  121.5 5.8 %copy-start.2 = (bf16[128,2048]{1,0:T(8,128)(2,1)S(1)}, bf16[128,2048]{1,0:T(8,128)(2,1)}, u32[]{:S(2)}) copy-start(bf16[128,2048]{1,0:T(8,128)(2,1)} %get-tuple-element.10) | copy-start | bytes 1572868

commit v3 on v2

--- a/solution.py
+++ b/solution.py
@@ -66,8 +66,8 @@
     act_hbm, cot_hbm, cache_hbm, length, buckets, new_bucket, ln_gain, norm_gain, frozen_hbm, query_hbm, wout_hbm, rab,
     out_ref, gsum_hbm, gtab_ref,
     act, cot, wts, rows, pre_slope, sent, proj, kv, bk_out, bks, onehot, bias, att, slope, wout, grad_gated, gated, grad_att,
-    tsum, gq_out, gq_in, grad_pre_t, rs_out, rs_in, ag_out, tab_one, tab_two,
-    loc_sem, kv_s, kv_r, bk_s, bk_r, g_s, g_r, pj_s, pj_r, w_s, w_r, px_s, px_r, p1_s, p1_r, p2_s, p2_r, p3_s, p3_r, gq_s, gq_r, rs_s, rs_r, ag_s, ag_r, t1_s, t1_r, t2_s, t2_r,
+    tsum, gq_out, gq_in, grad_pre_t, rs_out, r1_in, r2_out, r2_in, ag_buf, tab_one, tab_two,
+    loc_sem, kv_s, kv_r, bk_s, bk_r, g_s, g_r, pj_s, pj_r, w_s, w_r, px_s, px_r, p1_s, p1_r, p2_s, p2_r, p3_s, p3_r, gq_s, gq_r, r1_s, r1_r, r2_s, r2_r, a1_s, a1_r, a2_s, a2_r, t1_s, t1_r, t2_s, t2_r,
 ):
     h = lax.axis_index("history")
     d = lax.axis_index("dp")
@@ -344,16 +344,7 @@
             att[:, lanes] = total
         return carry
 
-    lax.fori_loop(0, DP // 2, attend, 0)
-    for step in plane_steps:
-        for copy in plane_two(*step):
-            copy.wait_recv()
-    for k in range(1, 4):
-        plane_share(k).start()
-    for i in (3, 4):
-        wring[i].wait_recv()
-        wring[i + 4].start()
-    lax.fori_loop(DP // 2, DP, attend, 0)
+    lax.fori_loop(0, DP, attend, 0)
 
     load_cot.wait()
     load_wout.wait()
@@ -365,22 +356,30 @@
             part = dot_nt(cot[:, lanes], wout[m, half, pl.ds(2 * n, 2)].reshape(512, COLS))
             grad_gated[:, cols] = part if first else grad_gated[:, cols] + part
 
+    for step in plane_steps:
+        for copy in plane_two(*step):
+            copy.wait_recv()
+    for k in range(1, 4):
+        plane_share(k).start()
     gated_part(d, 0, True)
     gated_part(d, 1, True)
     own_wout.wait_recv()
     gated_part(dpx(0, 1), 0)
     gated_part(dpx(0, 1), 1)
+    gated_part(dpx(3, 0), 1)
+    gated_part(dpx(1, 0), 1)
     for k in (3, 1, 2):
         gated_part(dpx(k, 0), 0)
     for k in (3, 1, 2):
         plane_share(k).wait_recv()
         gated_part(dpx(k, 1), 0)
-    gated_part(dpx(3, 0), 1)
-    gated_part(dpx(1, 0), 1)
     wring[5].wait_recv()
     gated_part(dpx(3, 1), 1)
     wring[6].wait_recv()
     gated_part(dpx(1, 1), 1)
+    for i in (3, 4):
+        wring[i].wait_recv()
+        wring[i + 4].start()
     gated_part(dpx(2, 0), 1)
     wring[7].wait_recv()
     wring[8].wait_recv()
@@ -425,9 +424,12 @@
         gq_out[k, m] = (total * SCALE).astype(BF16)
 
     def back_steps(half, first, stop):
-        def step(k, carry):
+        def step(i, carry):
+            k = 2 * i + 1
             attend_back(dpo(k), half)
+            attend_back(dpo(k + 1), half)
             gq_copy(half, k).start()
+            gq_copy(half, k + 1).start()
             return carry
 
         lax.fori_loop(first, stop, step, 0)
@@ -440,47 +442,94 @@
         lax.fori_loop(1, stop, step, 0)
 
     def own_back(half):
+        attend_back(dpo(DP - 1), half)
         attend_back(d, half)
+        gq_copy(half, DP - 1).start()
         gq_in[half, d] = gq_out[half, d]
-
-    def rs_copy(half, k):
-        to, i = hist(k), half * HIST + k
-        return remote(rs_out.at[half, to], rs_in.at[half, h], rs_s.at[i], rs_r.at[i], (to, d))
 
     def weight_half(half):
         run(gq_copy, DP, "wait_recv", half)
         for i in range(DP):
             pre = pre_slope[i, :, pl.ds(half * HEAD, HEAD)]
             grad_pre_t[half, :, pl.ds(i * TOK, TOK)] = (gq_in[half, i].astype(F32) * pre).astype(BF16).T
-        for kz in (1, 3, 2, 0):
-            to_z = lax.rem(z + kz, 4)
-            lanes = pl.ds(pl.multiple_of(to_z * 512, 512), 512)
-            piece = dot_nn(grad_pre_t[half], rows[:, :, lanes].reshape(DP * TOK, 512)).astype(BF16)
-            for j in range(4):
-                rs_out[half, to_z * 4 + j] = piece[:, j * TOK : (j + 1) * TOK]
-            for ky in (1, 0, 3, 2):
-                if kz or ky:
-                    rs_copy(half, kz * 4 + ky).start()
-        rs_in[half, h] = rs_out[half, h]
-
-    def ag_copy(half, k):
-        block = gsum_hbm.at[pl.ds(pl.multiple_of(h * TOK, TOK), TOK), pl.ds(half * HEAD, HEAD)]
-        i = half * HIST + k
-        return remote(ag_out.at[half], block, ag_s.at[i], ag_r.at[i], (hist(k), d))
-
-    def own_gsum(half):
-        block = gsum_hbm.at[pl.ds(pl.multiple_of(h * TOK, TOK), TOK), pl.ds(half * HEAD, HEAD)]
-        return pltpu.make_async_copy(ag_out.at[half], block, loc_sem.at[8 + half])
-
-    def gather_half(half):
-        run(rs_copy, HIST, "wait_recv", half)
-        total = rs_in[half, 0].astype(F32)
-        for i in range(1, HIST):
-            total = total + rs_in[half, i].astype(F32)
-        ag_out[half] = total.T.astype(BF16)
-        for k in LINK_ORDER:
-            ag_copy(half, k).start()
-        own_gsum(half).start()
+        for i in range(4):
+            piece = dot_nn(grad_pre_t[half], rows[:, :, pl.ds(i * 512, 512)].reshape(DP * TOK, 512)).astype(BF16)
+            rs_out[half, i] = piece.T.reshape(4, 2, HEAD // 2, HEAD)
+        for k in (1, 3, 2):
+            for side in range(2):
+                sum_one(half, side, k).start()
+
+    def along(side, k):
+        return (lax.rem(z + k, 4), y) if side == 0 else (z, lax.rem(y + k, 4))
+
+    def place(zy):
+        return (zy[0] * 4 + zy[1], d)
+
+    def line(ref, half, side, zy):
+        return ref.at[half, zy[0], :, side] if side == 0 else ref.at[half, :, zy[1], side]
+
+    def own(side):
+        return z if side == 0 else y
+
+    def sems(pair, half, side, k):
+        i = (half * 2 + side) * 4 + k
+        return pair[0].at[i], pair[1].at[i]
+
+    def sum_one(half, side, k):
+        to = along(side, k)
+        return remote(line(rs_out, half, side, to), r1_in.at[half, side, own(side)], *sems((r1_s, r1_r), half, side, k), place(to))
+
+    def sum_two(half, side, k):
+        to = along(1 - side, k)
+        src = r2_out.at[half, side, to[1 - side]]
+        return remote(src, r2_in.at[half, side, own(1 - side)], *sems((r2_s, r2_r), half, side, k), place(to))
+
+    def gather_one(half, side, k):
+        block = ag_buf.at[half, z, y, side]
+        return remote(block, block, *sems((a1_s, a1_r), half, side, k), place(along(1 - side, k)))
+
+    def gsum_line(half, side):
+        lanes = pl.ds(half * HEAD, HEAD)
+        return gsum_hbm.at[z, :, side, :, lanes] if side == 0 else gsum_hbm.at[:, y, side, :, lanes]
+
+    def gather_two(half, side, k):
+        src = line(ag_buf, half, side, (z, y))
+        return remote(src, gsum_line(half, side), *sems((a2_s, a2_r), half, side, k), place(along(side, k)))
+
+    def own_gsum(half, side):
+        return pltpu.make_async_copy(line(ag_buf, half, side, (z, y)), gsum_line(half, side), loc_sem.at[8 + half * 2 + side])
+
+    def after_one(half):
+        for side in range(2):
+            r1_in[half, side, own(side)] = rs_out[half, z, :, 0] if side == 0 else rs_out[half, :, y, 1]
+            for k in (1, 3, 2):
+                sum_one(half, side, k).wait_recv()
+            total = r1_in[half, side, 0].astype(F32)
+            for i in range(1, 4):
+                total = total + r1_in[half, side, i].astype(F32)
+            r2_out[half, side] = total
+            for k in (1, 3, 2):
+                sum_two(half, side, k).start()
+
+    def after_two(half):
+        for side in range(2):
+            r2_in[half, side, own(1 - side)] = r2_out[half, side, own(1 - side)]
+            for k in (1, 3, 2):
+                sum_two(half, side, k).wait_recv()
+            total = r2_in[half, side, 0]
+            for i in range(1, 4):
+                total = total + r2_in[half, side, i]
+            ag_buf[half, z, y, side] = total.astype(BF16)
+            for k in (1, 3, 2):
+                gather_one(half, side, k).start()
+
+    def after_three(half):
+        for side in range(2):
+            for k in (1, 3, 2):
+                gather_one(half, side, k).wait_recv()
+            for k in (1, 3, 2):
+                gather_two(half, side, k).start()
+            own_gsum(half, side).start()
 
     def out_cols(m, carry):
         lanes = pl.ds(pl.multiple_of(m * COLS, COLS), COLS)
@@ -494,11 +543,11 @@
     def t2_copy(k):
         return remote(tab_two.at[h], tab_two.at[h], t2_s.at[k], t2_r.at[k], (hist(k), d))
 
-    back_steps(0, 1, DP)
+    back_steps(0, 0, 3)
     own_back(0)
-    back_steps(1, 1, 4)
+    back_steps(1, 0, 2)
     weight_half(0)
-    back_steps(1, 4, DP)
+    back_steps(1, 2, 3)
     own_back(1)
 
     table = jnp.zeros((HEADS, BUCKETS), F32)
@@ -507,9 +556,11 @@
     tab_one[d] = table
     run(t1_copy, DP, "start")
 
-    lax.fori_loop(0, DP // 2, out_cols, 0)
+    lax.fori_loop(0, 2, out_cols, 0)
+    after_one(0)
     weight_half(1)
-    gather_half(0)
+    lax.fori_loop(2, 4, out_cols, 0)
+    after_two(0)
 
     run(t1_copy, DP, "wait_recv")
     table = tab_one[0]
@@ -518,8 +569,12 @@
     tab_two[h] = table
     run(t2_copy, HIST, "start")
 
-    lax.fori_loop(DP // 2, DP, out_cols, 0)
-    gather_half(1)
+    after_one(1)
+    lax.fori_loop(4, 6, out_cols, 0)
+    after_three(0)
+    after_two(1)
+    lax.fori_loop(6, DP, out_cols, 0)
+    after_three(1)
 
     run(t2_copy, HIST, "wait_recv")
     table = tab_two[0]
@@ -541,10 +596,12 @@
         run(copy, stop, "wait_send")
     for half in range(2):
         run(gq_copy, DP, "wait_send", half)
-        run(rs_copy, HIST, "wait_send", half)
-        run(ag_copy, HIST, "wait_recv", half)
-        run(ag_copy, HIST, "wait_send", half)
-        own_gsum(half).wait()
+        for side in range(2):
+            for k in (1, 3, 2):
+                for copy in (sum_one, sum_two, gather_one):
+                    copy(half, side, k).wait_send()
+                gather_two(half, side, k).wait()
+            own_gsum(half, side).wait()
 
 
 def layer(actions, cotangent, cache, length, buckets, new_bucket, ln_gain, norm_gain, w_frozen, w_query, w_out, rab):
@@ -552,12 +609,12 @@
     vmem = pl.BlockSpec(memory_space=pltpu.VMEM)
     smem = pl.BlockSpec(memory_space=pltpu.SMEM)
     dma = pltpu.SemaphoreType.DMA
-    sem_sizes = (10, KV_COPIES, KV_COPIES, HIST, HIST, 9, 9, DP, DP, 9, 9, 4, 4, 18, 18, 18, 18, 4, 4, 2 * DP, 2 * DP, 2 * HIST, 2 * HIST, 2 * HIST, 2 * HIST, DP, DP, HIST, HIST)
+    sem_sizes = (12, KV_COPIES, KV_COPIES, HIST, HIST, 9, 9, DP, DP, 9, 9, 4, 4, 18, 18, 18, 18, 4, 4, 2 * DP, 2 * DP, *[16] * 8, DP, DP, HIST, HIST)
     return pl.pallas_call(
         kernel,
         out_shape=(
             jax.ShapeDtypeStruct((TOK, WIDTH), BF16),
-            jax.ShapeDtypeStruct((WIDTH, COLS), BF16),
+            jax.ShapeDtypeStruct((4, 4, 2, HEAD // 2, COLS), BF16),
             jax.ShapeDtypeStruct((HEADS, BUCKETS), F32),
         ),
         in_specs=[any_space, any_space, any_space, smem, vmem, vmem, vmem, vmem, any_space, any_space, any_space, vmem],
@@ -585,9 +642,11 @@
             pltpu.VMEM((2, DP, TOK, HEAD), BF16),
             pltpu.VMEM((2, DP, TOK, HEAD), BF16),
             pltpu.VMEM((2, HEAD, DP * TOK), BF16),
-            pltpu.VMEM((2, HIST, HEAD, TOK), BF16),
-            pltpu.VMEM((2, HIST, HEAD, TOK), BF16),
-            pltpu.VMEM((2, TOK, HEAD), BF16),
+            pltpu.VMEM((2, 4, 4, 2, HEAD // 2, HEAD), BF16),
+            pltpu.VMEM((2, 2, 4, 4, HEAD // 2, HEAD), BF16),
+            pltpu.VMEM((2, 2, 4, HEAD // 2, HEAD), F32),
+            pltpu.VMEM((2, 2, 4, HEAD // 2, HEAD), F32),
+            pltpu.VMEM((2, 4, 4, 2, HEAD // 2, HEAD), BF16),
             pltpu.VMEM((DP, HEADS, BUCKETS), F32),
             pltpu.VMEM((HIST, HEADS, BUCKETS), F32),
         ]
@@ -615,7 +674,7 @@
         w_out.reshape(2, 4, 4, 2, 32, COLS),
         rab_table,
     )
-    query_new, query_m_new, query_v_new = adam_update(w_query, query_m, query_v, grad_sum.astype(F32))
+    query_new, query_m_new, query_v_new = adam_update(w_query, query_m, query_v, grad_sum.reshape(WIDTH, COLS).astype(F32))
     rab_new, rab_m_new, rab_v_new = adam_update(rab_table, rab_m, rab_v, grad_table)
     return (result.reshape(actions.shape), query_new, query_m_new, query_v_new, rab_new, rab_m_new, rab_v_new)
 

time: 129 us -> 126 us (0.977)
  Pallas kernels: 120 us -> 118 us
    pallas_call x1, Pallas kernels: 120 us -> 118 us  [layer(): pl.pallas_call(kernel, out_shape=(jax.ShapeDtypeStruct((TOK, WIDTH), BF16...]
where the time goes in v3:
time: 126 us
  Pallas kernels  118 us (94%)
  other arithmetic  5.76 us (5%)
  between operations  1.38 us (1%)
    pallas_call x1, Pallas kernels, layer(): pl.pallas_call(kernel, out_shape=(jax.ShapeDtypeStruct((TOK, WIDTH), BF16...  118 us
    convert_element_type x1, other arithmetic, adam_update(): return (stepped.astype(weight.dtype), first_new, second_new)  5.14 us

profile of v3, /device:TPU:0, one launch (start us, length us, event | category | flops | bytes accessed | tf_op | source)
XLA Modules:
  0.0 125.9 jit_solution(5288429411734660689)
XLA Ops:
  1.3 0.0 copy-start
  1.3 0.0 copy-start.1
  1.3 118.0 %layer.1 = (bf16[128,2048]{1,0:T(8,128)(2,1)}, bf16[4,4,2,64,256]{4,3,2,1,0:T(8,128)(2,1)}, f32[16,128]{1,0:T(8,128)}) custom-call(bf16[128,2048]{1,0:T(8,128)(2,1)} %bitcast.17, bf16[128,2048]{1,0:T(8,128)(2,1)} %bitcast.18, bf16[2,16,32,2048]{3,2,1,0:T(8,128)(2,1)} %bitcast.14, s32[1,1]{1,0:T(1,128)S(6)} %copy.24.length, s32[16,1,32]{2,1,0:T(1,128)} %buckets.1, ...), custom_call_target="tpu_custom_call" | custom-call | tf_op jit(solution)/shard_map/layer/pallas_call | solution.py:613
  119.3 0.0 copy-done
  119.3 0.0 copy-done.1
  119.3 0.0 copy-start.3
  119.3 0.0 copy-start.4
  119.3 0.0 copy-start.5
  119.3 0.0 copy-start.6
  119.3 0.0 copy-start.2
  119.3 5.1 %subtract_convert_fusion = (bf16[2048,256]{1,0:T(8,128)(2,1)}, f32[2048,256]{1,0:T(8,128)}, f32[2048,256]{1,0:T(8,128)}) fusion(bf16[2048,256]{1,0:T(8,128)(2,1)S(1)} %copy-done, bf16[4,4,2,64,256]{4,3,2,1,0:T(8,128)(2,1)} %get-tuple-element.11, f32[2048,256]{1,0:T(8,128)S(1)} %copy-done.1, f32[2048,256]{1,0:T(8,128)} %param.27), kind=kLoop, calls=%fused_computation.5 | loop fusion | flops 7340032 | bytes 11534336 | tf_op jit(solution)/shard_map/convert_element_type | solution.py:41
  124.5 0.0 copy-done.3
  124.5 0.0 copy-done.4
  124.5 0.0 copy-done.5
  124.5 0.0 copy-done.6
  124.5 0.6 divide_subtract_fusion
  125.1 0.0 copy-done.2
  125.1 0.8 copy.25
Async XLA Ops:
  1.3 118.0 %copy-start = (bf16[2048,256]{1,0:T(8,128)(2,1)S(1)}, bf16[2048,256]{1,0:T(8,128)(2,1)}, u32[]{:S(2)}) copy-start(bf16[2048,256]{1,0:T(8,128)(2,1)} %query_hbm.1) | copy-start | bytes 3145732
  1.3 118.0 %copy-start.1 = (f32[2048,256]{1,0:T(8,128)S(1)}, f32[2048,256]{1,0:T(8,128)}, u32[]{:S(2)}) copy-start(f32[2048,256]{1,0:T(8,128)} %param.26) | copy-start | bytes 6291460
  119.3 5.2 %copy-start.3 = (f32[16,128]{1,0:T(8,128)S(1)}, f32[16,128]{1,0:T(8,128)}, u32[]{:S(2)}) copy-start(f32[16,128]{1,0:T(8,128)} %rab.1) | copy-start | bytes 24580
  119.3 5.2 %copy-start.4 = (f32[16,128]{1,0:T(8,128)S(1)}, f32[16,128]{1,0:T(8,128)}, u32[]{:S(2)}) copy-start(f32[16,128]{1,0:T(8,128)} %param.30) | copy-start | bytes 24580
  119.3 5.2 %copy-start.5 = (f32[16,128]{1,0:T(8,128)S(1)}, f32[16,128]{1,0:T(8,128)}, u32[]{:S(2)}) copy-start(f32[16,128]{1,0:T(8,128)} %param.31) | copy-start | bytes 24580
  119.3 5.2 %copy-start.6 = (f32[16,128]{1,0:T(8,128)S(1)}, f32[16,128]{1,0:T(8,128)}, u32[]{:S(2)}) copy-start(f32[16,128]{1,0:T(8,128)} %get-tuple-element.12) | copy-start | bytes 24580
  119.3 5.8 %copy-start.2 = (bf16[128,2048]{1,0:T(8,128)(2,1)S(1)}, bf16[128,2048]{1,0:T(8,128)(2,1)}, u32[]{:S(2)}) copy-start(bf16[128,2048]{1,0:T(8,128)(2,1)} %get-tuple-element.10) | copy-start | bytes 1572868

commit v4 on v3

--- a/solution.py
+++ b/solution.py
@@ -65,9 +65,9 @@
 def kernel(
     act_hbm, cot_hbm, cache_hbm, length, buckets, new_bucket, ln_gain, norm_gain, frozen_hbm, query_hbm, wout_hbm, rab,
     out_ref, gsum_hbm, gtab_ref,
-    act, cot, wts, rows, pre_slope, sent, proj, kv, bk_out, bks, onehot, bias, att, slope, wout, grad_gated, gated, grad_att,
-    tsum, gq_out, gq_in, grad_pre_t, rs_out, r1_in, r2_out, r2_in, ag_buf, tab_one, tab_two,
-    loc_sem, kv_s, kv_r, bk_s, bk_r, g_s, g_r, pj_s, pj_r, w_s, w_r, px_s, px_r, p1_s, p1_r, p2_s, p2_r, p3_s, p3_r, gq_s, gq_r, r1_s, r1_r, r2_s, r2_r, a1_s, a1_r, a2_s, a2_r, t1_s, t1_r, t2_s, t2_r,
+    act, cot, wts, rows, pre_slope, sent, proj, kv, bk_out, bks, onehot, bias, att, slope, wout, grad_gated, gate_scaled, inverse_std, gated, grad_att,
+    tsum, gq_out, gq_in, grad_pre_t, rs_out, r1_in, r2_out, r2_in, ag_buf, tab_one, tab_two, tab_three,
+    loc_sem, kv_s, kv_r, bk_s, bk_r, g_s, g_r, pj_s, pj_r, w_s, w_r, px_s, px_r, p1_s, p1_r, p2_s, p2_r, p3_s, p3_r, gq_s, gq_r, r1_s, r1_r, r2_s, r2_r, a1_s, a1_r, a2_s, a2_r, t1_s, t1_r, t2_s, t2_r, t3_s, t3_r,
 ):
     h = lax.axis_index("history")
     d = lax.axis_index("dp")
@@ -113,6 +113,13 @@
     placed = jnp.where(lane // SLAB == y, jnp.concatenate([buckets[:, 0, :]] * 4, axis=1), 0)
     for u in range(HIST):
         bk_out[u] = jnp.broadcast_to(placed[u : u + 1, :], (8, TOK))
+
+    def run(copy, stop, what, *half):
+        def step(k, carry):
+            getattr(copy(*half, k), what)()
+            return carry
+
+        lax.fori_loop(1, stop, step, 0)
 
     load_act.wait()
 
@@ -346,6 +353,22 @@
 
     lax.fori_loop(0, DP, attend, 0)
 
+    def stat_rows(r, carry):
+        part = pl.ds(pl.multiple_of(r * 16, 16), 16)
+        values = att[part, :]
+        center = values - jnp.mean(values, axis=-1, keepdims=True)
+        inverse = lax.rsqrt(jnp.mean(center * center, axis=-1, keepdims=True) + NORM_EPS)
+        nhat = center * inverse
+        gate = jnp.concatenate([proj[m, part, pl.ds(COLS, COLS)] for m in range(DP)], axis=1).astype(F32)
+        scaled = gate * norm_gain[...]
+        att[part, :] = nhat
+        gate_scaled[part, :] = scaled
+        gated[part, :] = (nhat * scaled).astype(BF16)
+        inverse_std[part, :] = jnp.broadcast_to(inverse, (16, TOK))
+        return carry
+
+    lax.fori_loop(0, TOK // 16, stat_rows, 0)
+
     load_cot.wait()
     load_wout.wait()
 
@@ -355,6 +378,18 @@
             cols = pl.ds(half * 1024 + n * 512, 512)
             part = dot_nt(cot[:, lanes], wout[m, half, pl.ds(2 * n, 2)].reshape(512, COLS))
             grad_gated[:, cols] = part if first else grad_gated[:, cols] + part
+
+    run(bk_copy, HIST, "wait_send")
+    run(pj_copy, DP, "wait_send")
+    for i in range(1, KV_COPIES):
+        kv_copy(i).wait_send()
+    for copy in ring.values():
+        copy.wait_send()
+    for k in range(1, 4):
+        plane_x(k).wait_send()
+    for step in plane_steps:
+        for copy in plane_one(*step):
+            copy.wait_send()
 
     for step in plane_steps:
         for copy in plane_two(*step):
@@ -368,6 +403,9 @@
     gated_part(dpx(0, 1), 1)
     gated_part(dpx(3, 0), 1)
     gated_part(dpx(1, 0), 1)
+    for i in (3, 4):
+        wring[i].wait_recv()
+        wring[i + 4].start()
     for k in (3, 1, 2):
         gated_part(dpx(k, 0), 0)
     for k in (3, 1, 2):
@@ -377,9 +415,6 @@
     gated_part(dpx(3, 1), 1)
     wring[6].wait_recv()
     gated_part(dpx(1, 1), 1)
-    for i in (3, 4):
-        wring[i].wait_recv()
-        wring[i + 4].start()
     gated_part(dpx(2, 0), 1)
     wring[7].wait_recv()
     wring[8].wait_recv()
@@ -387,16 +422,10 @@
 
     def gate_rows(r, carry):
         part = pl.ds(pl.multiple_of(r * 16, 16), 16)
-        values = att[part, :]
-        center = values - jnp.mean(values, axis=-1, keepdims=True)
-        inverse = lax.rsqrt(jnp.mean(center * center, axis=-1, keepdims=True) + NORM_EPS)
-        nhat = center * inverse
-        gate = jnp.concatenate([proj[m, part, pl.ds(COLS, COLS)] for m in range(DP)], axis=1).astype(F32)
-        scaled = gate * norm_gain[...]
-        gated[part, :] = (nhat * scaled).astype(BF16)
-        grad_hat = grad_gated[part, :] * scaled
+        nhat = att[part, :]
+        grad_hat = grad_gated[part, :] * gate_scaled[part, :]
         along = jnp.mean(grad_hat * nhat, axis=-1, keepdims=True)
-        grad = inverse * (grad_hat - jnp.mean(grad_hat, axis=-1, keepdims=True) - nhat * along)
+        grad = inverse_std[part, 0:1] * (grad_hat - jnp.mean(grad_hat, axis=-1, keepdims=True) - nhat * along)
         grad_att[part, :] = grad.astype(BF16)
         return carry
 
@@ -434,13 +463,6 @@
 
         lax.fori_loop(first, stop, step, 0)
 
-    def run(copy, stop, what, *half):
-        def step(k, carry):
-            getattr(copy(*half, k), what)()
-            return carry
-
-        lax.fori_loop(1, stop, step, 0)
-
     def own_back(half):
         attend_back(dpo(DP - 1), half)
         attend_back(d, half)
@@ -541,7 +563,16 @@
         return remote(tab_one.at[d], tab_one.at[d], t1_s.at[k], t1_r.at[k], (h, dpo(k)))
 
     def t2_copy(k):
-        return remote(tab_two.at[h], tab_two.at[h], t2_s.at[k], t2_r.at[k], (hist(k), d))
+        return remote(tab_two.at[z], tab_two.at[z], t2_s.at[k], t2_r.at[k], place(along(0, k)))
+
+    def t3_copy(k):
+        return remote(tab_three.at[y], tab_three.at[y], t3_s.at[k], t3_r.at[k], place(along(1, k)))
+
+    def table_sum(ref, count):
+        total = ref[0]
+        for i in range(1, count):
+            total = total + ref[i]
+        return total
 
     back_steps(0, 0, 3)
     own_back(0)
@@ -560,40 +591,40 @@
     after_one(0)
     weight_half(1)
     lax.fori_loop(2, 4, out_cols, 0)
+    for copy in [*wring.values(), own_wout]:
+        copy.wait_send()
+    for k in range(1, 4):
+        plane_share(k).wait_send()
+    for step in plane_steps:
+        for copy in plane_two(*step):
+            copy.wait_send()
     after_two(0)
 
     run(t1_copy, DP, "wait_recv")
-    table = tab_one[0]
-    for i in range(1, DP):
-        table = table + tab_one[i]
-    tab_two[h] = table
-    run(t2_copy, HIST, "start")
+    tab_two[z] = table_sum(tab_one, DP)
+    for k in (1, 3, 2):
+        t2_copy(k).start()
 
     after_one(1)
     lax.fori_loop(4, 6, out_cols, 0)
     after_three(0)
     after_two(1)
+    for k in (1, 3, 2):
+        t2_copy(k).wait_recv()
+    tab_three[y] = table_sum(tab_two, 4)
+    for k in (1, 3, 2):
+        t3_copy(k).start()
     lax.fori_loop(6, DP, out_cols, 0)
     after_three(1)
 
-    run(t2_copy, HIST, "wait_recv")
-    table = tab_two[0]
-    for i in range(1, HIST):
-        table = table + tab_two[i]
-    gtab_ref[...] = table
-
-    for copy in [*ring.values(), *wring.values(), own_wout]:
-        copy.wait_send()
-    for k in range(1, 4):
-        plane_x(k).wait_send()
-        plane_share(k).wait_send()
-    for step in plane_steps:
-        for copy in plane_one(*step) + plane_two(*step):
-            copy.wait_send()
-    for i in range(1, KV_COPIES):
-        kv_copy(i).wait_send()
-    for copy, stop in ((bk_copy, HIST), (pj_copy, DP), (t1_copy, DP), (t2_copy, HIST)):
-        run(copy, stop, "wait_send")
+    for k in (1, 3, 2):
+        t3_copy(k).wait_recv()
+    gtab_ref[...] = table_sum(tab_three, 4)
+
+    run(t1_copy, DP, "wait_send")
+    for k in (1, 3, 2):
+        t2_copy(k).wait_send()
+        t3_copy(k).wait_send()
     for half in range(2):
         run(gq_copy, DP, "wait_send", half)
         for side in range(2):
@@ -609,7 +640,7 @@
     vmem = pl.BlockSpec(memory_space=pltpu.VMEM)
     smem = pl.BlockSpec(memory_space=pltpu.SMEM)
     dma = pltpu.SemaphoreType.DMA
-    sem_sizes = (12, KV_COPIES, KV_COPIES, HIST, HIST, 9, 9, DP, DP, 9, 9, 4, 4, 18, 18, 18, 18, 4, 4, 2 * DP, 2 * DP, *[16] * 8, DP, DP, HIST, HIST)
+    sem_sizes = (12, KV_COPIES, KV_COPIES, HIST, HIST, 9, 9, DP, DP, 9, 9, 4, 4, 18, 18, 18, 18, 4, 4, 2 * DP, 2 * DP, *[16] * 8, DP, DP, 4, 4, 4, 4)
     return pl.pallas_call(
         kernel,
         out_shape=(
@@ -636,6 +667,8 @@
             pltpu.VMEM((HEADS, TOK, KEYS), F32),
             pltpu.VMEM((DP, 2, 4, 4, 2, 32, COLS), BF16),
             pltpu.VMEM((TOK, WIDTH), F32),
+            pltpu.VMEM((TOK, WIDTH), F32),
+            pltpu.VMEM((TOK, TOK), F32),
             pltpu.VMEM((TOK, WIDTH), BF16),
             pltpu.VMEM((TOK, WIDTH), BF16),
             pltpu.VMEM((HEADS, 8, KEYS), F32),
@@ -648,12 +681,46 @@
             pltpu.VMEM((2, 2, 4, HEAD // 2, HEAD), F32),
             pltpu.VMEM((2, 4, 4, 2, HEAD // 2, HEAD), BF16),
             pltpu.VMEM((DP, HEADS, BUCKETS), F32),
-            pltpu.VMEM((HIST, HEADS, BUCKETS), F32),
+            pltpu.VMEM((4, HEADS, BUCKETS), F32),
+            pltpu.VMEM((4, HEADS, BUCKETS), F32),
         ]
         + [dma((n,)) for n in sem_sizes],
         compiler_params=pltpu.CompilerParams(collective_id=0, has_side_effects=True, vmem_limit_bytes=60 * 1024 * 1024),
         name="layer",
     )(actions, cotangent, cache, length, buckets, new_bucket, ln_gain, norm_gain, w_frozen, w_query, w_out, rab)
+
+
+ADAM_ROWS = 1024
+
+
+def adam_kernel(
+    grad, weight, moment_one, moment_two, table_grad, table, table_one, table_two, done,
+    weight_new, one_new, two_new, table_new, table_one_new, table_two_new, result,
+):
+    updated = adam_update(weight[...], moment_one[...], moment_two[...], grad[...].astype(F32))
+    weight_new[...], one_new[...], two_new[...] = updated
+    result[...] = done[...]
+
+    @pl.when(pl.program_id(0) == 0)
+    def _():
+        updated = adam_update(table[...], table_one[...], table_two[...], table_grad[...])
+        table_new[...], table_one_new[...], table_two_new[...] = updated
+
+
+def adam(grad, weight, moment_one, moment_two, table_grad, table, table_one, table_two, done):
+    steps = WIDTH // ADAM_ROWS
+    rows = pl.BlockSpec((ADAM_ROWS, COLS), lambda i: (i, 0))
+    small = pl.BlockSpec((HEADS, BUCKETS), lambda i: (0, 0))
+    tokens = pl.BlockSpec((TOK // steps, WIDTH), lambda i: (i, 0))
+    operands = (grad, weight, moment_one, moment_two, table_grad, table, table_one, table_two, done)
+    return pl.pallas_call(
+        adam_kernel,
+        grid=(steps,),
+        out_shape=[jax.ShapeDtypeStruct(a.shape, a.dtype) for a in operands[1:4] + operands[5:]],
+        in_specs=[rows] * 4 + [small] * 4 + [tokens],
+        out_specs=[rows] * 3 + [small] * 3 + [tokens],
+        name="adam",
+    )(*operands)
 
 
 def shards(
@@ -674,8 +741,9 @@
         w_out.reshape(2, 4, 4, 2, 32, COLS),
         rab_table,
     )
-    query_new, query_m_new, query_v_new = adam_update(w_query, query_m, query_v, grad_sum.reshape(WIDTH, COLS).astype(F32))
-    rab_new, rab_m_new, rab_v_new = adam_update(rab_table, rab_m, rab_v, grad_table)
+    query_new, query_m_new, query_v_new, rab_new, rab_m_new, rab_v_new, result = adam(
+        grad_sum.reshape(WIDTH, COLS), w_query, query_m, query_v, grad_table, rab_table, rab_m, rab_v, result
+    )
     return (result.reshape(actions.shape), query_new, query_m_new, query_v_new, rab_new, rab_m_new, rab_v_new)
 
 

time: 126 us -> 123 us (0.976)
  other arithmetic: 5.76 us -> 0 us
  Pallas kernels: 118 us -> 122 us
    pallas_call x0 -> x1, Pallas kernels: none -> 5.7 us  [adam(): pl.pallas_call(adam_kernel, grid=(steps,), out_shape=[jax.ShapeDtypeStruc...]
    convert_element_type x1 -> x0, other arithmetic: 5.14 us -> none  [adam_update(): return (stepped.astype(weight.dtype), first_new, second_new)]
    pallas_call x1, Pallas kernels: 118 us -> 116 us  [layer(): pl.pallas_call(kernel, out_shape=(jax.ShapeDtypeStruct((TOK, WIDTH), BF16...]
where the time goes in v4:
time: 123 us
  Pallas kernels  122 us (99%)
  between operations  1.29 us (1%)
    pallas_call x1, Pallas kernels, layer(): pl.pallas_call(kernel, out_shape=(jax.ShapeDtypeStruct((TOK, WIDTH), BF16...  116 us
    pallas_call x1, Pallas kernels, adam(): pl.pallas_call(adam_kernel, grid=(steps,), out_shape=[jax.ShapeDtypeStruc...  5.7 us

profile of v4, /device:TPU:0, one launch (start us, length us, event | category | flops | bytes accessed | tf_op | source)
XLA Modules:
  0.0 123.2 jit_solution(5002475845284146501)
XLA Ops:
  1.3 116.2 %layer.1 = (bf16[128,2048]{1,0:T(8,128)(2,1)}, bf16[4,4,2,64,256]{4,3,2,1,0:T(8,128)(2,1)}, f32[16,128]{1,0:T(8,128)}) custom-call(bf16[128,2048]{1,0:T(8,128)(2,1)} %bitcast.12, bf16[128,2048]{1,0:T(8,128)(2,1)} %bitcast.13, bf16[2,16,32,2048]{3,2,1,0:T(8,128)(2,1)} %bitcast.9, s32[1,1]{1,0:T(1,128)S(6)} %copy.23.length, s32[16,1,32]{2,1,0:T(1,128)} %buckets.1, ...), custom_call_target="tpu_custom_call" | custom-call | tf_op jit(solution)/shard_map/layer/pallas_call | solution.py:644
  117.5 5.7 %adam.1 = (bf16[2048,256]{1,0:T(8,128)(2,1)}, f32[2048,256]{1,0:T(8,128)}, f32[2048,256]{1,0:T(8,128)}, f32[16,128]{1,0:T(8,128)}, f32[16,128]{1,0:T(8,128)}, /*...) custom-call(bf16[2048,256]{1,0:T(8,128)(2,1)} %bitcast.10, bf16[2048,256]{1,0:T(8,128)(2,1)} %weight.1, ...), custom_call_target="tpu_custom_call" | custom-call | tf_op jit(solution)/shard_map/adam/pallas_call | solution.py:716

commit v5 on v4

--- a/solution.py
+++ b/solution.py
@@ -67,7 +67,7 @@
     out_ref, gsum_hbm, gtab_ref,
     act, cot, wts, rows, pre_slope, sent, proj, kv, bk_out, bks, onehot, bias, att, slope, wout, grad_gated, gate_scaled, inverse_std, gated, grad_att,
     tsum, gq_out, gq_in, grad_pre_t, rs_out, r1_in, r2_out, r2_in, ag_buf, tab_one, tab_two, tab_three,
-    loc_sem, kv_s, kv_r, bk_s, bk_r, g_s, g_r, pj_s, pj_r, w_s, w_r, px_s, px_r, p1_s, p1_r, p2_s, p2_r, p3_s, p3_r, gq_s, gq_r, r1_s, r1_r, r2_s, r2_r, a1_s, a1_r, a2_s, a2_r, t1_s, t1_r, t2_s, t2_r, t3_s, t3_r,
+    loc_sem, kv_s, kv_r, bk_s, bk_r, g_s, g_r, pj_s, pj_r, w_s, w_r, px_s, px_r, p1_s, p1_r, p2_s, p2_r, p3_s, p3_r, gq_s, gq_r, r1_s, r1_r, r2_s, r2_r, a2_s, a2_r, t1_s, t1_r, t2_s, t2_r, t3_s, t3_r,
 ):
     h = lax.axis_index("history")
     d = lax.axis_index("dp")
@@ -502,13 +502,8 @@
         return remote(line(rs_out, half, side, to), r1_in.at[half, side, own(side)], *sems((r1_s, r1_r), half, side, k), place(to))
 
     def sum_two(half, side, k):
-        to = along(1 - side, k)
-        src = r2_out.at[half, side, to[1 - side]]
-        return remote(src, r2_in.at[half, side, own(1 - side)], *sems((r2_s, r2_r), half, side, k), place(to))
-
-    def gather_one(half, side, k):
-        block = ag_buf.at[half, z, y, side]
-        return remote(block, block, *sems((a1_s, a1_r), half, side, k), place(along(1 - side, k)))
+        src, dst = r2_out.at[half, side], r2_in.at[half, side, own(1 - side)]
+        return remote(src, dst, *sems((r2_s, r2_r), half, side, k), place(along(1 - side, k)))
 
     def gsum_line(half, side):
         lanes = pl.ds(half * HEAD, HEAD)
@@ -529,26 +524,22 @@
             total = r1_in[half, side, 0].astype(F32)
             for i in range(1, 4):
                 total = total + r1_in[half, side, i].astype(F32)
-            r2_out[half, side] = total
+            r2_out[half, side] = total.astype(BF16)
             for k in (1, 3, 2):
                 sum_two(half, side, k).start()
 
     def after_two(half):
         for side in range(2):
-            r2_in[half, side, own(1 - side)] = r2_out[half, side, own(1 - side)]
+            r2_in[half, side, own(1 - side)] = r2_out[half, side]
             for k in (1, 3, 2):
                 sum_two(half, side, k).wait_recv()
-            total = r2_in[half, side, 0]
+            total = r2_in[half, side, 0].astype(F32)
             for i in range(1, 4):
-                total = total + r2_in[half, side, i]
-            ag_buf[half, z, y, side] = total.astype(BF16)
-            for k in (1, 3, 2):
-                gather_one(half, side, k).start()
-
-    def after_three(half):
-        for side in range(2):
-            for k in (1, 3, 2):
-                gather_one(half, side, k).wait_recv()
+                total = total + r2_in[half, side, i].astype(F32)
+            if side == 0:
+                ag_buf[half, z, :, 0] = total.astype(BF16)
+            else:
+                ag_buf[half, :, y, 1] = total.astype(BF16)
             for k in (1, 3, 2):
                 gather_two(half, side, k).start()
             own_gsum(half, side).start()
@@ -607,7 +598,6 @@
 
     after_one(1)
     lax.fori_loop(4, 6, out_cols, 0)
-    after_three(0)
     after_two(1)
     for k in (1, 3, 2):
         t2_copy(k).wait_recv()
@@ -615,7 +605,6 @@
     for k in (1, 3, 2):
         t3_copy(k).start()
     lax.fori_loop(6, DP, out_cols, 0)
-    after_three(1)
 
     for k in (1, 3, 2):
         t3_copy(k).wait_recv()
@@ -629,7 +618,7 @@
         run(gq_copy, DP, "wait_send", half)
         for side in range(2):
             for k in (1, 3, 2):
-                for copy in (sum_one, sum_two, gather_one):
+                for copy in (sum_one, sum_two):
                     copy(half, side, k).wait_send()
                 gather_two(half, side, k).wait()
             own_gsum(half, side).wait()
@@ -640,7 +629,7 @@
     vmem = pl.BlockSpec(memory_space=pltpu.VMEM)
     smem = pl.BlockSpec(memory_space=pltpu.SMEM)
     dma = pltpu.SemaphoreType.DMA
-    sem_sizes = (12, KV_COPIES, KV_COPIES, HIST, HIST, 9, 9, DP, DP, 9, 9, 4, 4, 18, 18, 18, 18, 4, 4, 2 * DP, 2 * DP, *[16] * 8, DP, DP, 4, 4, 4, 4)
+    sem_sizes = (12, KV_COPIES, KV_COPIES, HIST, HIST, 9, 9, DP, DP, 9, 9, 4, 4, 18, 18, 18, 18, 4, 4, 2 * DP, 2 * DP, *[16] * 6, DP, DP, 4, 4, 4, 4)
     return pl.pallas_call(
         kernel,
         out_shape=(
@@ -677,8 +666,8 @@
             pltpu.VMEM((2, HEAD, DP * TOK), BF16),
             pltpu.VMEM((2, 4, 4, 2, HEAD // 2, HEAD), BF16),
             pltpu.VMEM((2, 2, 4, 4, HEAD // 2, HEAD), BF16),
-            pltpu.VMEM((2, 2, 4, HEAD // 2, HEAD), F32),
-            pltpu.VMEM((2, 2, 4, HEAD // 2, HEAD), F32),
+            pltpu.VMEM((2, 2, 4, HEAD // 2, HEAD), BF16),
+            pltpu.VMEM((2, 2, 4, 4, HEAD // 2, HEAD), BF16),
             pltpu.VMEM((2, 4, 4, 2, HEAD // 2, HEAD), BF16),
             pltpu.VMEM((DP, HEADS, BUCKETS), F32),
             pltpu.VMEM((4, HEADS, BUCKETS), F32),

time: 123 us -> 122 us (level)
    pallas_call x1, Pallas kernels: 116 us -> 115 us  [layer(): pl.pallas_call(kernel, out_shape=(jax.ShapeDtypeStruct((TOK, WIDTH), BF16...]
where the time goes in v5:
time: 122 us
  Pallas kernels  121 us (99%)
  between operations  1.29 us (1%)
    pallas_call x1, Pallas kernels, layer(): pl.pallas_call(kernel, out_shape=(jax.ShapeDtypeStruct((TOK, WIDTH), BF16...  115 us
    pallas_call x1, Pallas kernels, adam(): pl.pallas_call(adam_kernel, grid=(steps,), out_shape=[jax.ShapeDtypeStruc...  5.7 us

profile of v5, /device:TPU:0, one launch (start us, length us, event | category | flops | bytes accessed | tf_op | source)
XLA Modules:
  0.0 121.9 jit_solution(2121258380609497355)
XLA Ops:
  1.3 114.9 %layer.1 = (bf16[128,2048]{1,0:T(8,128)(2,1)}, bf16[4,4,2,64,256]{4,3,2,1,0:T(8,128)(2,1)}, f32[16,128]{1,0:T(8,128)}) custom-call(bf16[128,2048]{1,0:T(8,128)(2,1)} %bitcast.12, bf16[128,2048]{1,0:T(8,128)(2,1)} %bitcast.13, bf16[2,16,32,2048]{3,2,1,0:T(8,128)(2,1)} %bitcast.9, s32[1,1]{1,0:T(1,128)S(6)} %copy.23.length, s32[16,1,32]{2,1,0:T(1,128)} %buckets.1, ...), custom_call_target="tpu_custom_call" | custom-call | tf_op jit(solution)/shard_map/layer/pallas_call | solution.py:633
  116.2 5.7 %adam.1 = (bf16[2048,256]{1,0:T(8,128)(2,1)}, f32[2048,256]{1,0:T(8,128)}, f32[2048,256]{1,0:T(8,128)}, f32[16,128]{1,0:T(8,128)}, f32[16,128]{1,0:T(8,128)}, /*...) custom-call(bf16[2048,256]{1,0:T(8,128)(2,1)} %bitcast.10, bf16[2048,256]{1,0:T(8,128)(2,1)} %weight.1, ...), custom_call_target="tpu_custom_call" | custom-call | tf_op jit(solution)/shard_map/adam/pallas_call | solution.py:705

commit v6 on v5

--- a/solution.py
+++ b/solution.py
@@ -582,6 +582,21 @@
     after_one(0)
     weight_half(1)
     lax.fori_loop(2, 4, out_cols, 0)
+    after_two(0)
+
+    run(t1_copy, DP, "wait_recv")
+    tab_two[z] = table_sum(tab_one, DP)
+    for k in (1, 3, 2):
+        t2_copy(k).start()
+
+    after_one(1)
+    for k in (1, 3, 2):
+        t2_copy(k).wait_recv()
+    tab_three[y] = table_sum(tab_two, 4)
+    for k in (1, 3, 2):
+        t3_copy(k).start()
+    lax.fori_loop(4, 6, out_cols, 0)
+    after_two(1)
     for copy in [*wring.values(), own_wout]:
         copy.wait_send()
     for k in range(1, 4):
@@ -589,21 +604,6 @@
     for step in plane_steps:
         for copy in plane_two(*step):
             copy.wait_send()
-    after_two(0)
-
-    run(t1_copy, DP, "wait_recv")
-    tab_two[z] = table_sum(tab_one, DP)
-    for k in (1, 3, 2):
-        t2_copy(k).start()
-
-    after_one(1)
-    lax.fori_loop(4, 6, out_cols, 0)
-    after_two(1)
-    for k in (1, 3, 2):
-        t2_copy(k).wait_recv()
-    tab_three[y] = table_sum(tab_two, 4)
-    for k in (1, 3, 2):
-        t3_copy(k).start()
     lax.fori_loop(6, DP, out_cols, 0)
 
     for k in (1, 3, 2):
@@ -686,8 +686,14 @@
     grad, weight, moment_one, moment_two, table_grad, table, table_one, table_two, done,
     weight_new, one_new, two_new, table_new, table_one_new, table_two_new, result,
 ):
-    updated = adam_update(weight[...], moment_one[...], moment_two[...], grad[...].astype(F32))
-    weight_new[...], one_new[...], two_new[...] = updated
+    gradient = grad[...].astype(F32)
+    first = BETA_ONE * moment_one[...] + (1.0 - BETA_ONE) * gradient
+    second = BETA_TWO * moment_two[...] + (1.0 - BETA_TWO) * gradient * gradient
+    one_new[...] = first
+    two_new[...] = second
+    root = second * lax.rsqrt(second)
+    stepped = weight[...].astype(F32) - LEARN_RATE * first * pl.reciprocal(root + ADAM_EPS)
+    weight_new[...] = stepped.astype(BF16)
     result[...] = done[...]
 
     @pl.when(pl.program_id(0) == 0)

time: 122 us -> 122 us (level)
  no operation moved by 1% of the time
where the time goes in v6:
time: 122 us
  Pallas kernels  120 us (98%)
  between operations  1.29 us (1%)
    pallas_call x1, Pallas kernels, layer(): pl.pallas_call(kernel, out_shape=(jax.ShapeDtypeStruct((TOK, WIDTH), BF16...  115 us
    pallas_call x1, Pallas kernels, adam(): pl.pallas_call(adam_kernel, grid=(steps,), out_shape=[jax.ShapeDtypeStruc...  5.41 us

profile of v6, /device:TPU:0, one launch (start us, length us, event | category | flops | bytes accessed | tf_op | source)
XLA Modules:
  0.0 121.5 jit_solution(2161517069519038584)
XLA Ops:
  1.3 114.8 %layer.1 = (bf16[128,2048]{1,0:T(8,128)(2,1)}, bf16[4,4,2,64,256]{4,3,2,1,0:T(8,128)(2,1)}, f32[16,128]{1,0:T(8,128)}) custom-call(bf16[128,2048]{1,0:T(8,128)(2,1)} %bitcast.12, bf16[128,2048]{1,0:T(8,128)(2,1)} %bitcast.13, bf16[2,16,32,2048]{3,2,1,0:T(8,128)(2,1)} %bitcast.9, s32[1,1]{1,0:T(1,128)S(6)} %copy.23.length, s32[16,1,32]{2,1,0:T(1,128)} %buckets.1, ...), custom_call_target="tpu_custom_call" | custom-call | tf_op jit(solution)/shard_map/layer/pallas_call | solution.py:633
  116.1 5.4 %adam.1 = (bf16[2048,256]{1,0:T(8,128)(2,1)}, f32[2048,256]{1,0:T(8,128)}, f32[2048,256]{1,0:T(8,128)}, f32[16,128]{1,0:T(8,128)}, f32[16,128]{1,0:T(8,128)}, /*...) custom-call(bf16[2048,256]{1,0:T(8,128)(2,1)} %bitcast.10, bf16[2048,256]{1,0:T(8,128)(2,1)} %weight.1, ...), custom_call_target="tpu_custom_call" | custom-call | tf_op jit(solution)/shard_map/adam/pallas_call | solution.py:711

commit v7 on v6

--- a/solution.py
+++ b/solution.py
@@ -429,7 +429,7 @@
         grad_att[part, :] = grad.astype(BF16)
         return carry
 
-    lax.fori_loop(0, TOK // 16, gate_rows, 0)
+    lax.fori_loop(0, TOK // 16, gate_rows, 0, unroll=2)
 
     def gq_copy(half, k):
         to, i = dpo(k), half * DP + k

time: 122 us -> 121 us (level)
  no operation moved by 1% of the time
where the time goes in v7:
time: 121 us
  Pallas kernels  120 us (99%)
  between operations  1.29 us (1%)
    pallas_call x1, Pallas kernels, layer(): pl.pallas_call(kernel, out_shape=(jax.ShapeDtypeStruct((TOK, WIDTH), BF16...  114 us
    pallas_call x1, Pallas kernels, adam(): pl.pallas_call(adam_kernel, grid=(steps,), out_shape=[jax.ShapeDtypeStruc...  5.41 us

profile of v7, /device:TPU:0, one launch (start us, length us, event | category | flops | bytes accessed | tf_op | source)
XLA Modules:
  0.0 121.2 jit_solution(1538522383188600626)
XLA Ops:
  1.3 114.5 %layer.1 = (bf16[128,2048]{1,0:T(8,128)(2,1)}, bf16[4,4,2,64,256]{4,3,2,1,0:T(8,128)(2,1)}, f32[16,128]{1,0:T(8,128)}) custom-call(bf16[128,2048]{1,0:T(8,128)(2,1)} %bitcast.12, bf16[128,2048]{1,0:T(8,128)(2,1)} %bitcast.13, bf16[2,16,32,2048]{3,2,1,0:T(8,128)(2,1)} %bitcast.9, s32[1,1]{1,0:T(1,128)S(6)} %copy.23.length, s32[16,1,32]{2,1,0:T(1,128)} %buckets.1, ...), custom_call_target="tpu_custom_call" | custom-call | tf_op jit(solution)/shard_map/layer/pallas_call | solution.py:633
  115.8 5.4 %adam.1 = (bf16[2048,256]{1,0:T(8,128)(2,1)}, f32[2048,256]{1,0:T(8,128)}, f32[2048,256]{1,0:T(8,128)}, f32[16,128]{1,0:T(8,128)}, f32[16,128]{1,0:T(8,128)}, /*...) custom-call(bf16[2048,256]{1,0:T(8,128)(2,1)} %bitcast.10, bf16[2048,256]{1,0:T(8,128)(2,1)} %weight.1, ...), custom_call_target="tpu_custom_call" | custom-call | tf_op jit(solution)/shard_map/adam/pallas_call | solution.py:711
